TPU v7x, 256 devices: a whole 4x4x8 slice. The times are simulated.
256 devices in a mesh: dp: 8 (over y, core), tensor: 32 (over x, z).
Axes of the slice: x: 4, y: 4, z: 8, core: 2. Of those that a mesh axis runs over, the one named last changes fastest.
Arguments:
- hidden: bfloat16 [8192, 2048], P(('dp', 'tensor')), parts along dimension 0, may hold values from -6 to 6
- norm_gain: bfloat16 [2048], replicated, may hold values from 0.099609375 to 1.8984375
- router_weight: bfloat16 [2048, 8], replicated, may hold values from -0.125 to 0.125
- kv_weight: bfloat16 [2048, 4096], P(None, 'tensor'), may hold values from -0.125 to 0.125
- query_weight: bfloat16 [2048, 16384], P(None, 'tensor'), may hold values from -0.125 to 0.125
- out_weight: bfloat16 [16384, 2048], P('tensor'), may hold values from -0.5 to 0.5
- routes: int32 [8192, 2], P('dp'), parts along dimension 0, may hold values from 0 to 7, all different within a row; in each aligned block of 1024 rows (0 to 1023, 1024 to 2047, ...) at most 384 rows name the same one
- segment_ids: int32 [8192], P('dp'), parts along dimension 0, may hold values from 0 to 3, never falling along the last dimension, each value on 1 to 512 neighbouring positions
- page_table: int32 [64], P('dp'), parts along dimension 0, may hold values from 0 to 15, as said below
- kv_cache: bfloat16 [128, 128, 4096], P('dp', None, 'tensor'), parts along dimension 0, may hold values from -6 to 6
Outputs:
- attended_out: bfloat16 [8192, 2048], P(('dp', 'tensor')), parts along dimension 0
- new_cache: bfloat16 [128, 128, 4096], P('dp', None, 'tensor'), parts along dimension 0
There are 8 independent parts, one for each index of `dp`. A program takes and returns all parts, laid end to end along the dimension named above; an argument that names none is the same for every part. Nothing has to cross between parts.
Inputs may be any that keep to these rules, and one draw needn't show every extreme that they name: `routes`: no expert is named by more than 384 tokens of a batch, and one is named by exactly 384; a token names two different experts. `segment_ids`: ids never fall along the pack; each prompt has 1 to 512 tokens and one has exactly 512. `page_table`: distinct pages.
All inputs are finite; a program needn't handle non-finite values.
Results may differ from a plain program's by a relative error of at most 0.025.
Values may be sent and summed in bfloat16 or wider, within the bound.
A program may use at most 128 MiB of HBM per device.

v0:
```python
import jax
import jax.numpy as jnp
from jax import lax
from jax.sharding import PartitionSpec as P

D = 2048
HD = 128
EA = 8
PAGE = 128


def swapped(array, axis, bit):
    return lax.ppermute(array, axis, [(i, i ^ 1 << bit) for i in range(lax.axis_size(axis))])


def normalize(hidden, norm_gain):
    values = hidden.astype(jnp.float32)
    factor = lax.rsqrt(jnp.mean(values * values, axis=-1, keepdims=True) + 1e-05)
    return (values * factor * norm_gain.astype(jnp.float32)).astype(jnp.bfloat16)


def gate_table(normed, router_weight, routes):
    logits = jnp.dot(normed, router_weight, preferred_element_type=jnp.float32)
    chosen = jnp.take_along_axis(logits, routes, axis=1)
    weights = jax.nn.softmax(chosen, axis=-1)
    expert_ids = jnp.arange(router_weight.shape[1], dtype=jnp.int32)
    onehot = (routes[:, :, None] == expert_ids[None, None, :]).astype(jnp.float32)
    return jnp.sum(weights[:, :, None] * onehot, axis=1)


def positions_of(segment_ids):
    index_row = jnp.arange(segment_ids.shape[0], dtype=jnp.int32)
    starts_here = jnp.concatenate([jnp.ones((1,), dtype=bool), segment_ids[1:] != segment_ids[:-1]])
    segment_start = lax.cummax(jnp.where(starts_here, index_row, 0), axis=0)
    return index_row - segment_start


def rotate(values, positions):
    half_width = values.shape[-1] // 2
    frequency = 10000.0 ** (-jnp.arange(half_width, dtype=jnp.float32) / half_width)
    angles = positions.astype(jnp.float32)[:, None] * frequency[None, :]
    angles = angles.reshape((values.shape[0],) + (1,) * (values.ndim - 2) + (half_width,))
    cosine = jnp.cos(angles)
    sine_part = jnp.sin(angles)
    leading = values[..., :half_width]
    trailing = values[..., half_width:]
    return jnp.concatenate(
        [leading * cosine - trailing * sine_part, trailing * cosine + leading * sine_part], axis=-1
    )


def expert_slots(routes, expert, capacity):
    is_hit = jnp.any(routes == expert, axis=1)
    running = jnp.cumsum(is_hit.astype(jnp.int32))
    placed = jnp.where(is_hit, running - 1, capacity)
    index_row = jnp.arange(routes.shape[0], dtype=jnp.int32)
    slot_tok = jnp.zeros((capacity + 1,), jnp.int32).at[placed].set(index_row)[:capacity]
    is_valid = jnp.arange(capacity, dtype=jnp.int32) < running[-1]
    return (slot_tok, is_valid)


def attend(queries, key_rows, value_rows, allowed):
    scores = jnp.dot(queries, key_rows.T, preferred_element_type=jnp.float32)
    scores = jnp.where(allowed, scores, -1e30)
    probabilities = jax.nn.softmax(scores, axis=-1).astype(jnp.bfloat16)
    return jnp.dot(probabilities, value_rows, preferred_element_type=jnp.float32)


def project_kv(normed, weight, positions, first_block):
    projected = jnp.dot(normed, weight, preferred_element_type=jnp.float32)
    block_total = weight.shape[1] // HD
    blocks = projected.reshape(normed.shape[0], block_total, HD)
    block_index = first_block + jnp.arange(block_total, dtype=jnp.int32)
    turned = rotate(blocks, positions)
    chosen = jnp.where((block_index % 2 == 0)[None, :, None], turned, blocks)
    return chosen.astype(jnp.bfloat16).reshape(normed.shape[0], weight.shape[1])


def local(
    hidden,
    norm_gain,
    router_weight,
    kv_weight,
    query_weight,
    out_weight,
    routes,
    segment_ids,
    page_table,
    kv_cache,
):
    device_index = lax.axis_index("tensor")
    token_count = routes.shape[0]
    capacity = 3 * token_count // 8
    normed = lax.all_gather(normalize(hidden, norm_gain), "tensor", axis=0, tiled=True)
    gates = gate_table(normed, router_weight, routes)
    positions = positions_of(segment_ids)
    kv_width = kv_weight.shape[1]
    block_count = kv_width // HD
    own_rows = project_kv(normed, kv_weight, positions, device_index * block_count)
    new_cache = kv_cache.at[page_table].set(own_rows.reshape(page_table.shape[0], PAGE, kv_width))
    partner_rows = swapped(own_rows, "tensor", 0)
    leading_first = device_index % 2 == 0
    head_rows = jnp.where(
        leading_first,
        jnp.concatenate([own_rows, partner_rows], axis=1),
        jnp.concatenate([partner_rows, own_rows], axis=1),
    )
    local_heads = head_rows.shape[1] // (2 * HD)
    head_rows = head_rows.reshape(token_count, local_heads, 2, HD)
    pair_count = query_weight.shape[1] // HD
    local_experts = pair_count // local_heads
    query_cols = query_weight.reshape(D, local_heads, local_experts, HD)
    index_row = jnp.arange(token_count, dtype=jnp.int32)
    scale_factor = HD ** (-0.5)
    spread = jnp.zeros((token_count, local_heads, local_experts, HD), jnp.bfloat16)
    for expert_slot in range(local_experts):
        expert = (device_index * pair_count + expert_slot) % EA
        slot_tok, is_valid = expert_slots(routes, expert, capacity)
        queries = jnp.einsum(
            "cd,dhk->chk",
            normed[slot_tok],
            query_cols[:, :, expert_slot],
            preferred_element_type=jnp.float32,
        )
        queries = (rotate(queries, positions[slot_tok]) * scale_factor).astype(jnp.bfloat16)
        allowed = (segment_ids[slot_tok][:, None] == segment_ids[None, :]) & (
            index_row[None, :] <= slot_tok[:, None]
        )
        attended = jnp.stack(
            [attend(queries[:, 0], head_rows[:, 0, 0], head_rows[:, 0, 1], allowed)], axis=1
        )
        gate_here = gates[slot_tok, expert] * is_valid.astype(jnp.float32)
        gated = (attended * gate_here[:, None, None]).astype(jnp.bfloat16)
        target = jnp.where(is_valid, slot_tok, token_count)
        spread = spread.at[target, :, expert_slot].set(gated, mode="drop")
    flat_spread = spread.reshape(token_count, pair_count * HD)
    reduced = lax.psum_scatter(
        jnp.dot(flat_spread, out_weight, preferred_element_type=jnp.float32).astype(jnp.bfloat16),
        "tensor",
        scatter_dimension=0,
        tiled=True,
    ).astype(jnp.float32)
    attended_out = (hidden.astype(jnp.float32) + reduced).astype(jnp.bfloat16)
    return (attended_out, new_cache)


def solution(mesh):
    placed = (
        P(("dp", "tensor"), None),
        P(),
        P(),
        P(None, "tensor"),
        P(None, "tensor"),
        P("tensor", None),
        P("dp", None),
        P("dp"),
        P("dp"),
        P("dp", None, "tensor"),
    )
    return jax.shard_map(
        local,
        mesh=mesh,
        in_specs=placed,
        out_specs=(P(("dp", "tensor"), None), P("dp", None, "tensor")),
        check_vma=False,
    )
```

profile of v0, /device:TPU:8, one launch (start us, length us, event | category | flops | bytes accessed | tf_op | source)
XLA Modules:
  0.0 492.9 jit_solution(13262688912807085128)
XLA Ops:
  7.2 0.8 convert_element_type.154
  8.1 1.0 fusion.27
  9.1 1.7 fusion.29
  14.0 4.3 scatter_custom_fusion.6
  18.3 1.1 shift-left_or_fusion
  19.4 3.0 gather_fusion.12
  22.6 1.9 gather_fusion.14
  24.5 4.3 scatter_custom_fusion.4
  28.8 1.3 shift-left_or_fusion.1
  30.1 1.9 gather_fusion.10
  32.0 3.0 gather_fusion.8
  36.9 4.3 scatter_custom_fusion.2
  41.2 1.2 shift-left_or_fusion.2
  42.4 1.9 gather_fusion.6
  44.3 3.0 gather_fusion.4
  48.0 4.5 scatter_custom_fusion
  52.5 1.2 shift-left_or_fusion.3
  53.7 1.9 gather_fusion.2
  55.6 3.0 gather_fusion
  58.6 3.9 copy.62
  67.8 28.1 %all-gather.2.cloned.1.call-done = bf16[1024,2048]{1,0:T(8,128)(2,1)} async-done(((bf16[32,2048]{1,0:T(8,128)(2,1)}), bf16[1024,2048]{1,0:T(8,128)(2,1)}) %all-gather.2.cloned.1.call-update) | async-done | bytes 4194320 | tf_op jit(solution)/shard_map/all_gather | solution.py:94
  95.9 7.8 %gather_fusion.13 = bf16[384,2048]{1,0:T(8,128)(2,1)} fusion(bf16[1024,2048]{1,0:T(8,128)(2,1)} %all-gather.2.cloned.1.call-done, s32[1024]{0:T(1024)S(1)} %pad_clamp_fusion), kind=kCustom, calls=%fused_computation.13 | custom fusion | bytes 3147264 | tf_op jit(solution)/shard_map/gather | solution.py:121
  103.7 2.8 convolution_bitcast_fusion
  106.5 7.8 %gather_fusion.9 = bf16[384,2048]{1,0:T(8,128)(2,1)} fusion(bf16[1024,2048]{1,0:T(8,128)(2,1)} %all-gather.2.cloned.1.call-done, s32[1024]{0:T(1024)S(1)} %pad_clamp_fusion.1), kind=kCustom, calls=%fused_computation.9 | custom fusion | bytes 3147264 | tf_op jit(solution)/shard_map/gather | solution.py:121
  114.2 2.9 convolution_bitcast_fusion.1
  117.1 3.9 fusion.110
  121.0 1.2 fusion.24
  122.9 2.0 collective-permute-start
  124.9 1.2 fusion.111
  126.1 12.5 %gather_fusion.16 = f32[2048]{0:T(1024)S(1)} fusion(f32[1024,8]{0,1:T(8,128)S(1)} %fusion.111, s32[2048]{0:T(1024)S(1)} %reshape.1033), kind=kCustom, calls=%fused_computation.16 | custom fusion | bytes 32768 | tf_op jit(solution)/shard_map/jit(take_along_axis)/gather | solution.py:24
  139.5 2.7 gather_fusion.15
  142.7 2.7 gather_fusion.11
  146.1 2.7 gather_fusion.7
  149.5 7.8 %gather_fusion.1 = bf16[384,2048]{1,0:T(8,128)(2,1)} fusion(bf16[1024,2048]{1,0:T(8,128)(2,1)} %all-gather.2.cloned.1.call-done, s32[1024]{0:T(1024)S(1)} %copy-done.24), kind=kCustom, calls=%fused_computation.1 | custom fusion | bytes 3147264 | tf_op jit(solution)/shard_map/gather | solution.py:121
  157.2 2.1 convolution_bitcast_fusion.3
  159.4 2.7 gather_fusion.3
  163.2 7.8 %gather_fusion.5 = bf16[384,2048]{1,0:T(8,128)(2,1)} fusion(bf16[1024,2048]{1,0:T(8,128)(2,1)} %all-gather.2.cloned.1.call-done, s32[1024]{0:T(1024)S(1)} %copy-done.22), kind=kCustom, calls=%fused_computation.5 | custom fusion | bytes 3147264 | tf_op jit(solution)/shard_map/gather | solution.py:121
  171.0 2.2 convolution_bitcast_fusion.2
  173.2 1.5 fusion.52
  174.8 1.4 maximum_select_fusion.1
  183.1 19.3 %scatter_fusion = bf16[1024,4,128]{2,1,0:T(4,128)(2,1)S(1)} fusion(bf16[1024,4,128]{2,1,0:T(4,128)(2,1)S(1)} %broadcast.766, s32[384]{0:T(512)S(1)} %copy-done.7, bf16[384,128]{1,0:T(8,128)(2,1)S(1)} %fusion.12), kind=kCustom, calls=%fused_computation.18 | custom fusion | bytes 297984 | tf_op jit(solution)/shard_map/scatter | solution.py:135
  202.4 19.8 %scatter_fusion.1 = bf16[1024,4,128]{2,1,0:T(4,128)(2,1)S(1)} fusion(bf16[1024,4,128]{2,1,0:T(4,128)(2,1)S(1)} %scatter_fusion, s32[384]{0:T(512)S(1)} %copy-done.6, bf16[384,128]{1,0:T(8,128)(2,1)S(1)} %fusion.13), kind=kCustom, calls=%fused_computation.20 | custom fusion | bytes 297984 | tf_op jit(solution)/shard_map/scatter | solution.py:135
  222.2 19.5 %scatter_fusion.2 = bf16[1024,4,128]{2,1,0:T(4,128)(2,1)S(1)} fusion(bf16[1024,4,128]{2,1,0:T(4,128)(2,1)S(1)} %scatter_fusion.1, s32[384]{0:T(512)S(1)} %copy-done.5, bf16[384,128]{1,0:T(8,128)(2,1)S(1)} %fusion.14), kind=kCustom, calls=%fused_computation.22 | custom fusion | bytes 297984 | tf_op jit(solution)/shard_map/scatter | solution.py:135
  241.8 19.9 %scatter_fusion.3 = bf16[1024,4,128]{2,1,0:T(4,128)(2,1)S(1)} fusion(bf16[1024,4,128]{2,1,0:T(4,128)(2,1)S(1)} %scatter_fusion.2, s32[384]{0:T(512)S(1)} %copy-done.4, bf16[384,128]{1,0:T(8,128)(2,1)S(1)} %fusion.15), kind=kCustom, calls=%fused_computation.24 | custom fusion | bytes 297984 | tf_op jit(solution)/shard_map/scatter | solution.py:135
  261.6 4.3 convolution_convert_fusion
  266.6 1.1 copy.70
  268.5 215.5 %reduce-scatter.2.cloned.1.call-done = bf16[32,2048]{1,0:T(8,128)(2,1)} async-done(((bf16[1024,2048]{1,0:T(8,128)(2,1)}), bf16[32,2048]{1,0:T(8,128)(2,1)}) %reduce-scatter.2.cloned.1.call-update) | async-done | bytes 131088 | tf_op jit(solution)/shard_map/reduce_scatter | solution.py:137
  484.0 1.6 fusion.30
  (171 shorter events, 23.8 us)
Async XLA Ops:
  7.2 254.5 %copy-start = (bf16[512,2048]{1,0:T(8,128)(2,1)S(1)}, bf16[512,2048]{1,0:T(8,128)(2,1)}, u32[]{:S(2)}) copy-start(bf16[512,2048]{1,0:T(8,128)(2,1)} %param.15) | copy-start | bytes 6291460
  7.2 3.7 copy-start.18
  7.2 6.2 %copy-start.1 = (s32[1024]{0:T(1024)S(1)}, s32[1024]{0:T(1024)}, u32[]{:S(2)}) copy-start(s32[1024]{0:T(1024)} %param.17) | copy-start | bytes 12292
  7.2 88.7 %all-gather.2.cloned.1.call-start = ((), (), s32[]{:S(2)}) async-start(), calls=%async_computation.1 | async-start | bytes 4325376 | tf_op jit(solution)/shard_map/all_gather | solution.py:94
  10.8 473.2 %reduce-scatter.2.cloned.1.call-start = ((), (), s32[]{:S(2)}) async-start(), calls=%async_computation.2 | async-start | bytes 4325376 | tf_op jit(solution)/shard_map/reduce_scatter | solution.py:137
  42.4 4.9 %copy-start.21 = (s32[1024]{0:T(1024)}, s32[1024]{0:T(1024)S(1)}, u32[]{:S(2)}) copy-start(s32[1024]{0:T(1024)S(1)} %pad_clamp_fusion.2) | copy-start | bytes 12292
  53.7 4.9 copy-start.23
  67.8 53.2 %copy-start.29 = (f32[64]{0:T(128)}, f32[64]{0:T(128)S(1)}, u32[]{:S(2)}) copy-start(f32[64]{0:T(128)S(1)} %multiply_power_fusion) | copy-start | bytes 772
  114.2 2.9 copy-start.15
  117.1 7.8 %copy-start.3 = (bf16[1024,2048]{1,0:T(8,128)(2,1)S(1)}, bf16[1024,2048]{1,0:T(8,128)(2,1)}, u32[]{:S(2)}) copy-start(bf16[1024,2048]{1,0:T(8,128)(2,1)} %all-gather.2.cloned.1.call-done) | copy-start | bytes 12582916
  121.0 4.0 copy-start.20
  122.9 51.8 %collective-permute-start = (bf16[1024,128]{0,1:T(8,128)(2,1)}, bf16[1024,128]{0,1:T(8,128)(2,1)}, u32[]{:S(2)}, u32[]{:S(2)}) collective-permute-start(bf16[1024,128]{0,1:T(8,128)(2,1)} %fusion.18), channel_id=1, source_target_pairs={{0,1},{1,0},{2,3},{3,2},{4,5},{5,4},{6,7},{7,6},{8,9},{9,8},{10,11... | collective-permute-start | bytes 786440 | tf_op jit(solution)/shard_map/ppermute | solution.py:13
  126.1 13.2 %copy-start.19 = (s32[1024,2]{0,1:T(2,128)S(1)}, s32[1024,2]{0,1:T(2,128)}, u32[]{:S(2)}) copy-start(s32[1024,2]{0,1:T(2,128)} %param.16) | copy-start | bytes 24580
  126.1 13.3 %copy-start.8 = (s32[384]{0:T(512)S(1)}, s32[384]{0:T(512)}, u32[]{:S(2)}) copy-start(s32[384]{0:T(512)} %get-tuple-element.28) | copy-start | bytes 4612
  139.1 3.6 copy-start.9
  142.2 4.0 copy-start.10
  145.4 4.0 copy-start.24
  157.2 2.1 copy-start.11
  159.4 3.4 copy-start.28
  159.4 3.4 copy-start.30
  159.4 3.8 copy-start.22
  171.0 2.2 copy-start.16
  171.0 2.2 copy-start.17
  171.0 2.2 copy-start.25
  171.0 2.2 copy-start.26
  171.0 2.2 copy-start.27
  173.2 3.0 copy-start.2
  173.2 3.0 copy-start.31
  173.2 3.0 copy-start.35
  177.3 0.7 copy-start.32
  177.3 0.7 copy-start.36
  179.0 0.7 copy-start.33
  179.0 0.7 copy-start.37
  180.7 0.7 copy-start.34
  180.7 0.7 copy-start.38
  182.4 0.8 copy-start.7
  182.8 19.6 %copy-start.6 = (s32[384]{0:T(512)S(1)}, s32[384]{0:T(512)}, u32[]{:S(2)}) copy-start(s32[384]{0:T(512)} %fusion.83) | copy-start | bytes 4612
  183.1 39.1 %copy-start.5 = (s32[384]{0:T(512)S(1)}, s32[384]{0:T(512)}, u32[]{:S(2)}) copy-start(s32[384]{0:T(512)} %fusion.85) | copy-start | bytes 4612
  202.4 39.3 %copy-start.4 = (s32[384]{0:T(512)S(1)}, s32[384]{0:T(512)}, u32[]{:S(2)}) copy-start(s32[384]{0:T(512)} %fusion.87) | copy-start | bytes 4612
  265.9 0.7 copy-start.39
  265.9 1.8 copy-start.14
  265.9 218.1 %copy-start.12 = (bf16[32,2048]{1,0:T(8,128)(2,1)S(1)}, bf16[32,2048]{1,0:T(8,128)(2,1)}, u32[]{:S(2)}) copy-start(bf16[32,2048]{1,0:T(8,128)(2,1)} %param.10) | copy-start | bytes 393220
  268.5 217.2 %copy-start.13 = (bf16[16,128,128]{2,1,0:T(8,128)(2,1)}, bf16[16,128,128]{2,1,0:T(8,128)(2,1)S(1)}, u32[]{:S(2)}) copy-start(bf16[16,128,128]{2,1,0:T(8,128)(2,1)S(1)} %scatter_fusion.4) | copy-start | bytes 1572868
Sparse Core Ops, SparseCore 0:
  11.2 84.6 all-gather.1
  266.0 217.9 reduce-scatter.1
where the time goes:
time: 499 us; the launch traced here: 493 us
  waiting for transfers between devices  244 us (49%)
  local copies, waits for them, and re-layouts  182 us (36%)
  other arithmetic  26.6 us (5%)
  matrix products  23.4 us (5%)
  between operations  15.3 us (3%)
    reduce_scatter x1, waiting for transfers between devices, local(): lax.psum_scatter(jnp.dot(flat_spread, out_weight, preferred_element_type=...  216 us
    scatter x4, local copies, waits for them, and re-layouts, local(): spread = spread.at[target, :, expert_slot].set(gated, mode='drop')  78.4 us
    gather x4, local copies, waits for them, and re-layouts, local(): normed[slot_tok]  31.1 us
    all_gather x1, waiting for transfers between devices, local(): lax.all_gather(normalize(hidden, norm_gain), 'tensor', axis=0, tiled=True)  28.1 us
    scatter x4, local copies, waits for them, and re-layouts, expert_slots(): jnp.zeros((capacity + 1,), jnp.int32).at[placed].set(index_row)[:capacity]  17.4 us
    gather x5, local copies, waits for them, and re-layouts, gate_table(): chosen = jnp.take_along_axis(logits, routes, axis=1)  13.7 us
    gather x4, local copies, waits for them, and re-layouts, local(): segment_ids[slot_tok][:, None] == segment_ids[None, :]  12.1 us
    gather x4, local copies, waits for them, and re-layouts, local(): gate_here = gates[slot_tok, expert] * is_valid.astype(jnp.float32)  10.7 us
  transfers between devices with their start and end apart: 3, of which 2 were waited for; matrix products, arithmetic and copies ran while one was open for 22% of the time, Pallas kernels for 0%

commit v1 on v0

v1 whole, which is shorter than its diff:
```python
import functools

import jax
import jax.numpy as jnp
import numpy as np
from jax import lax
from jax.experimental import pallas as pl
from jax.experimental.pallas import tpu as pltpu
from jax.sharding import PartitionSpec as P

NX, NZ, ROWS, D, HD = 4, 8, 32, 2048, 128
EXPERTS = 4
HALF = ROWS // 2
X_OFFSETS = (0, -1, 1, -2)
Z_OFFSETS = (0, -1, 1, -2, 2, -3, 3, -4)
SEND_US, LATENCY_US = 1.31, 1.0


def gather_tasks():
    tasks = []
    for half in "AB":
        for i in X_OFFSETS:
            for j in Z_OFFSETS:
                sends = []
                if half == "A":
                    if j == 0 and i in (0, -1):
                        sends.append(("x+", (half, i - 1, 0)))
                    if j == 0 and i == 0:
                        sends.append(("x-", (half, 1, 0)))
                if -4 < j <= 0 and (half == "A" or i == 0):
                    sends.append(("z+", (half, i, j - 1)))
                if 0 <= j < 3 and (half == "A" or i == 0):
                    sends.append(("z-", (half, i, j + 1)))
                if half == "B":
                    if i in (0, -1):
                        sends.append(("x+", (half, i - 1, j)))
                    if i == 0:
                        sends.append(("x-", (half, 1, j)))
                own = i == 0 and j == 0
                tasks.append(
                    dict(
                        name=("recv", half, i, j),
                        deps=[] if own else [(half, i, j)],
                        after=[("norm",)] if own else [],
                        sends=sends,
                        block=(half, i, j),
                        cost=0.05,
                    )
                )
    return tasks


def reduce_tasks():
    tasks = []

    def add(half, i, j, deps, sends, cost):
        tasks.append(
            dict(name=("sum", half, i, j, len(tasks)), deps=deps, after=[("attend", i)], sends=sends, block=(half, i, j), cost=cost)
        )

    for i in (2, -1, 1, 0):
        for k in (4, 3, 2, 1):
            add("A", i, k, [("A", "L", i, k)] if k < 4 else [], [("z+", ("A", "L", i, k - 1))], 0.1)
        for k in (-3, -2, -1):
            add("A", i, k, [("A", "S", i, k)] if k > -3 else [], [("z-", ("A", "S", i, k + 1))], 0.1)
        deps = [("A", "L", i, 0), ("A", "S", i, 0)]
        if i == 1:
            deps.append(("A", "X", 1))
        if i == 0:
            deps += [("A", "X", 0), ("A", "Y", 0)]
        sends = {2: [("x+", ("A", "X", 1))], -1: [("x-", ("A", "Y", 0))], 1: [("x+", ("A", "X", 0))], 0: []}[i]
        add("A", i, 0, deps, sends, 0.15)
    for j in (4, -3, 3, -2, 2, -1, 1, 0):
        add("B", 2, j, [], [("x+", ("B", "L", 1, j))], 0.1)
        add("B", -1, j, [], [("x-", ("B", "S", 0, j))], 0.1)
        add("B", 1, j, [("B", "L", 1, j)], [("x+", ("B", "L", 0, j))], 0.1)
        deps = [("B", "L", 0, j), ("B", "S", 0, j)]
        sends = []
        if j > 0:
            deps += [("B", "Z", j)] if j < 4 else []
            sends = [("z+", ("B", "Z", j - 1))]
        elif j < 0:
            deps += [("B", "W", j)] if j > -3 else []
            sends = [("z-", ("B", "W", j + 1))]
        else:
            deps += [("B", "Z", 0), ("B", "W", 0)]
        add("B", 0, j, deps, sends, 0.15)
    return tasks


def compute_tasks():
    tasks = [dict(name=("norm",), after=[], cost=1.0)]
    tasks += [dict(name=("setup", n), after=[], cost=1.0) for n in range(4)]
    for j in Z_OFFSETS:
        after = [("recv", half, i, j) for half in "AB" for i in X_OFFSETS] + [("setup", n) for n in range(4)]
        tasks.append(dict(name=("project", j), after=after, cost=0.9))
    everything = [("project", j) for j in Z_OFFSETS]
    tasks.append(dict(name=("swap",), after=everything, cost=1.5))
    for i in (2, -1, 1, 0):
        tasks.append(dict(name=("attend", i), after=[("swap",)], cost=2.0))
    tasks.append(dict(name=("cache",), after=[("swap",), ("attend", 0)], cost=1.0))
    return tasks


@functools.cache
def plan():
    moves, work = gather_tasks() + reduce_tasks(), compute_tasks()
    clock, done, arrived, free, order = 0.0, set(), {}, {}, []
    while moves or work:
        best = None
        for task in moves:
            if all(a in done for a in task["after"]) and all(d in arrived for d in task["deps"]):
                at = max([arrived[d] for d in task["deps"]], default=0.0)
                if best is None or at < best[0]:
                    best = (at, task)
        ready = best is not None and best[0] <= clock
        task = None
        if not ready:
            task = next((w for w in work if all(a in done for a in w["after"])), None)
        if task is None:
            clock, task = max(clock, best[0]), best[1]
            moves.remove(task)
        else:
            work.remove(task)
        clock += task["cost"]
        for link, key in task.get("sends", []):
            begin = max(clock, free.get(link, 0.0))
            free[link] = begin + SEND_US
            arrived[key] = begin + SEND_US + LATENCY_US
        done.add(task["name"])
        order.append(task)
    return order, clock


GATHER_KEYS = [t["block"] for t in gather_tasks() if t["deps"]]
REDUCE_KEYS = [key for t in reduce_tasks() for _, key in t["sends"]]


def layer(
    hidden, gain, router, kv_weight, query_weight, out_weight, routes, segments, frequency, pages, cache,
    out, new_cache,
    full, part, landed, weight, out_w, pool, kv, query, cosine, sine, route, gate, mixed,
    gather_send, gather_recv, reduce_send, reduce_recv, kv_send, kv_recv, load, store,
):
    me = lax.axis_index("tensor")
    turn = 1 - 2 * lax.rem(lax.axis_index("dp"), 2)
    x, z = me // NZ, lax.rem(me, NZ)
    parity = lax.rem(z, 2)
    base = parity * EXPERTS

    def fx(i):
        return lax.rem(x + turn * i + NX, NX)

    def fz(j):
        return lax.rem(z + turn * j + NZ, NZ)

    links = {
        "x+": fx(1) * NZ + z,
        "x-": fx(-1) * NZ + z,
        "z+": x * NZ + fz(1),
        "z-": x * NZ + fz(-1),
    }
    partner = x * NZ + z + 1 - 2 * parity

    barrier = pltpu.get_barrier_semaphore()
    for device in links.values():
        pl.semaphore_signal(barrier, inc=1, device_id={"tensor": device}, device_id_type=pl.DeviceIdType.MESH)

    loads = [
        pltpu.make_async_copy(query_weight, weight.at[:, 0:512], load.at[0]),
        pltpu.make_async_copy(kv_weight, weight.at[:, 512:640], load.at[1]),
        pltpu.make_async_copy(out_weight, out_w, load.at[2]),
        pltpu.make_async_copy(cache, pool, load.at[3]),
    ]
    for copy in loads:
        copy.start()

    def rows_of(half):
        return pl.ds(0 if half == "A" else HALF, HALF)

    def remote(src, dst, send, recv, device):
        return pltpu.make_async_remote_copy(
            src_ref=src, dst_ref=dst, send_sem=send, recv_sem=recv,
            device_id={"tensor": device}, device_id_type=pl.DeviceIdType.MESH,
        )

    lane = lax.broadcasted_iota(jnp.int32, (128, 128), 1)
    sub = lax.broadcasted_iota(jnp.int32, (128, 128), 0)
    low = lane < HD // 2
    waiting = []

    def norm():
        values = hidden[...].astype(jnp.float32)
        factor = lax.rsqrt(jnp.mean(values * values, axis=-1, keepdims=True) + 1e-05)
        full[z, x] = (values * factor * gain[...].astype(jnp.float32)).astype(jnp.bfloat16)
        pl.semaphore_wait(barrier, 4)

    def setup(n):
        seg = segments[...]
        starts = [jnp.sum((seg < s).astype(jnp.float32), axis=1, keepdims=True) for s in (1, 2, 3)]
        for b in (2 * n, 2 * n + 1):
            token = (sub + b * 128).astype(jnp.float32)
            start = jnp.zeros_like(token)
            for s in starts:
                start = jnp.maximum(start, jnp.where(token >= s, s, 0.0))
            first = routes[0:1, b * 128 : b * 128 + 128].astype(jnp.float32)
            second = routes[1:2, b * 128 : b * 128 + 128].astype(jnp.float32)
            columns = jnp.where(sub == 0, first, jnp.where(sub == 1, second, 0.0)).T
            at = (b // 2, pl.ds(b % 2 * 4, 4))
            route[at] = jnp.where(lane == 2, start, columns).reshape(4, 32, 128)
            angle = (token - start) * frequency[...]
            k = jnp.floor(angle * 0.6366197723675814 + 0.5)
            r = angle - k * 1.5703125
            r = r - k * 4.837512969970703e-4
            r = r - k * 7.549789954891882e-8
            w = r * r
            sin = r + r * w * (-1.6666654611e-1 + w * (8.3321608736e-3 - w * 1.9515295891e-4))
            cos = 1.0 - 0.5 * w + w * w * (4.166664568298827e-2 + w * (-1.388731625493765e-3 + w * 2.443315711809948e-5))
            quarter = k - 4.0 * jnp.floor(k * 0.25)
            odd = (quarter == 1.0) | (quarter == 3.0)
            c = jnp.where(odd, sin, cos)
            s = jnp.where(odd, cos, sin)
            c = jnp.where((quarter == 1.0) | (quarter == 2.0), -c, c)
            s = jnp.where(quarter >= 2.0, -s, s)
            cosine[at] = c.reshape(4, 32, 128)
            sine[at] = jnp.where(low, -s, s).reshape(4, 32, 128)
        for c in range(4 * n, 4 * n + 4):
            block = router[:, c * 128 : c * 128 + 128].astype(jnp.float32)
            block = jnp.concatenate([block, jnp.zeros((120, 128), jnp.float32)], axis=0)
            weight[c * 128 : c * 128 + 128, 640:768] = block.T.astype(jnp.bfloat16)
        if n == 0:
            kv[:, 0:2] = jnp.zeros((2, 2, NZ, ROWS, HD), jnp.bfloat16)
        if n == 3:
            for copy in loads:
                copy.wait()

    def rotate(values, c, s):
        return values * c + pltpu.roll(values, HD // 2, 1) * s

    def project(j):
        za = fz(j)
        at = (slice(None), pl.ds(za, 1))
        made = jnp.dot(full[za].reshape(128, D), weight[...], preferred_element_type=jnp.float32)
        picks = route[at].reshape(128, 128)
        c, s = cosine[at].reshape(128, 128), sine[at].reshape(128, 128)
        for n in range(2):
            local = picks[:, n : n + 1] - base.astype(jnp.float32)
            values = jnp.zeros((128, HD), jnp.float32)
            for e in range(EXPERTS):
                values = jnp.where(local == float(e), made[:, e * HD : e * HD + HD], values)
            values = rotate(values, c, s) * (HD**-0.5)
            query[(n, *at)] = values.astype(jnp.bfloat16).reshape(4, 1, 32, 128)
        own = made[:, 512:640]
        own = jnp.where(parity == 0, rotate(own, c, s), own)
        kv[parity, 2:6, pl.ds(za, 1)] = own.astype(jnp.bfloat16).reshape(4, 1, 32, 128)
        logits = made[:, 640:768]
        lanes = lane.astype(jnp.float32)
        first = jnp.sum(jnp.where(lanes == picks[:, 0:1], logits, 0.0), axis=1, keepdims=True)
        second = jnp.sum(jnp.where(lanes == picks[:, 1:2], logits, 0.0), axis=1, keepdims=True)
        top = jnp.maximum(first, second)
        first, second = jnp.exp(first - top), jnp.exp(second - top)
        total = first + second
        gate[at] = jnp.where(lane == 0, first / total, second / total).reshape(4, 1, 32, 128)
        place = kv.at[parity, 2:6, za]
        copy = remote(place, place, kv_send.at[j % NZ], kv_recv.at[j % NZ], partner)
        copy.start()
        waiting.append(copy)

    def swap():
        for j in Z_OFFSETS:
            zp = lax.rem(z + 1 - 2 * parity + turn * j + NZ, NZ)
            place = kv.at[1 - parity, 2:6, zp]
            remote(place, place, kv_send.at[j % NZ], kv_recv.at[j % NZ], partner).wait_recv()

    def attend(i):
        xa = fx(i)
        for half in range(2):
            at = (xa, pl.ds(half * 4, 4))
            keys = kv[0, pl.ds(xa, 3)].reshape(768, HD)[half * 128 : half * 128 + 640]
            values = kv[1, pl.ds(xa, 3)].reshape(768, HD)[half * 128 : half * 128 + 640]
            q = jnp.concatenate([query[(n, *at)].reshape(128, HD) for n in range(2)], axis=0)
            scores = lax.dot_general(q, keys, (((1,), (1,)), ((), ())), preferred_element_type=jnp.float32)
            picks = route[at].reshape(128, 128)
            gates = gate[at].reshape(128, 128)
            token = lax.broadcasted_iota(jnp.int32, (128, 640), 0) + (xa * 256 + half * 128)
            index = lax.broadcasted_iota(jnp.int32, (128, 640), 1) + ((xa - 2) * 256 + half * 128)
            allowed = (index <= token) & (index >= picks[:, 2:3].astype(jnp.int32))
            results = []
            for n in range(2):
                score = jnp.where(allowed, scores[n * 128 : n * 128 + 128], -1e30)
                shifted = jnp.exp(score - jnp.max(score, axis=1, keepdims=True))
                total = jnp.sum(shifted, axis=1, keepdims=True)
                mean = jnp.dot(shifted.astype(jnp.bfloat16), values, preferred_element_type=jnp.float32) / total
                results.append(mean * gates[:, n : n + 1])
            local = [picks[:, n : n + 1] - base.astype(jnp.float32) for n in range(2)]
            for e in range(EXPERTS):
                pair = jnp.where(local[0] == float(e), results[0], jnp.where(local[1] == float(e), results[1], 0.0))
                mixed[half * 128 : half * 128 + 128, e * HD : e * HD + HD] = pair.astype(jnp.bfloat16)
        for n in range(0, D, 512):
            made = jnp.dot(mixed[...], out_w[:, n : n + 512], preferred_element_type=jnp.float32)
            part[xa, :, :, n : n + 512] = made.astype(jnp.bfloat16).reshape(NZ, ROWS, 512)

    def update_cache():
        def page(p, _):
            content = pool[p].astype(jnp.float32)
            for b in range(8):
                rows = kv[parity, 2 + b // 2, pl.ds(b % 2 * 4, 4)].reshape(128, HD).astype(jnp.float32)
                hit = jnp.full((128, 128), pages[b] - p, jnp.int32) == 0
                content = jnp.where(hit, rows, content)
            pool[p] = content.astype(jnp.bfloat16)
            return 0

        lax.fori_loop(0, 16, page, 0)
        copy = pltpu.make_async_copy(pool, new_cache, store)
        copy.start()
        return copy

    def receive(task):
        half, i, j = task["block"]
        place = full.at[fz(j), fx(i), rows_of(half)]
        if task["deps"]:
            n = GATHER_KEYS.index(task["deps"][0])
            remote(place, place, gather_send.at[n], gather_recv.at[n], me).wait_recv()
        for link, key in task["sends"]:
            n = GATHER_KEYS.index(key)
            copy = remote(place, place, gather_send.at[n], gather_recv.at[n], links[link])
            copy.start()
            waiting.append(copy)

    def combine(task):
        half, i, j = task["block"]
        at = (fx(i), fz(j), rows_of(half))
        slots = [REDUCE_KEYS.index(key) for key in task["deps"]]
        for n in slots:
            remote(landed.at[n], landed.at[n], reduce_send.at[n], reduce_recv.at[n], me).wait_recv()
        if slots:
            total = part[at].astype(jnp.float32)
            for n in slots:
                total = total + landed[n].astype(jnp.float32)
            if not task["sends"]:
                total = total + hidden[rows_of(half), :].astype(jnp.float32)
                out[rows_of(half), :] = total.astype(jnp.bfloat16)
            else:
                part[at] = total.astype(jnp.bfloat16)
        for link, key in task["sends"]:
            n = REDUCE_KEYS.index(key)
            copy = remote(part.at[at], landed.at[n], reduce_send.at[n], reduce_recv.at[n], links[link])
            copy.start()
            waiting.append(copy)

    stored = None
    for task in plan()[0]:
        kind, *rest = task["name"]
        if kind == "recv":
            receive(task)
        elif kind == "sum":
            combine(task)
        elif kind == "cache":
            stored = update_cache()
        else:
            dict(norm=norm, setup=setup, project=project, swap=swap, attend=attend)[kind](*rest)
    for copy in waiting:
        copy.wait_send()
    stored.wait()


def local(hidden, gain, router, kv_weight, query_weight, out_weight, routes, segments, pages, cache):
    half = HD // 2
    frequency = (10000.0 ** (-np.arange(half, dtype=np.float32) / np.float32(half))).astype(np.float32)
    frequency = np.concatenate([frequency, frequency])[None]
    vmem = pl.BlockSpec(memory_space=pltpu.VMEM)
    anywhere = pl.BlockSpec(memory_space=pl.ANY)
    dma = pltpu.SemaphoreType.DMA
    return pl.pallas_call(
        layer,
        out_shape=(
            jax.ShapeDtypeStruct(hidden.shape, jnp.bfloat16),
            jax.ShapeDtypeStruct(cache.shape, jnp.bfloat16),
        ),
        in_specs=[vmem] * 3 + [anywhere] * 3 + [vmem] * 3 + [pl.BlockSpec(memory_space=pltpu.SMEM), anywhere],
        out_specs=(vmem, anywhere),
        scratch_shapes=[
            pltpu.VMEM((NZ, NX, ROWS, D), jnp.bfloat16),
            pltpu.VMEM((NX, NZ, ROWS, D), jnp.bfloat16),
            pltpu.VMEM((len(REDUCE_KEYS), HALF, D), jnp.bfloat16),
            pltpu.VMEM((D, 768), jnp.bfloat16),
            pltpu.VMEM((512, D), jnp.bfloat16),
            pltpu.VMEM((16, 128, HD), jnp.bfloat16),
            pltpu.VMEM((2, NX + 2, NZ, ROWS, HD), jnp.bfloat16),
            pltpu.VMEM((2, NX, NZ, ROWS, HD), jnp.bfloat16),
            pltpu.VMEM((NX, NZ, ROWS, HD), jnp.float32),
            pltpu.VMEM((NX, NZ, ROWS, HD), jnp.float32),
            pltpu.VMEM((NX, NZ, ROWS, HD), jnp.float32),
            pltpu.VMEM((NX, NZ, ROWS, HD), jnp.float32),
            pltpu.VMEM((256, 512), jnp.bfloat16),
            dma((len(GATHER_KEYS),)),
            dma((len(GATHER_KEYS),)),
            dma((len(REDUCE_KEYS),)),
            dma((len(REDUCE_KEYS),)),
            dma((NZ,)),
            dma((NZ,)),
            dma((4,)),
            dma(()),
        ],
        compiler_params=pltpu.CompilerParams(
            collective_id=0, has_side_effects=True, vmem_limit_bytes=52 * 1024 * 1024
        ),
        name="layer",
    )(
        hidden, gain.reshape(1, D), router.T, kv_weight, query_weight, out_weight, routes.T,
        segments.reshape(1, -1), jnp.asarray(frequency), pages, cache,
    )


def solution(mesh):
    placed = (
        P(("dp", "tensor"), None),
        P(),
        P(),
        P(None, "tensor"),
        P(None, "tensor"),
        P("tensor", None),
        P("dp", None),
        P("dp"),
        P("dp"),
        P("dp", None, "tensor"),
    )
    return jax.shard_map(
        local,
        mesh=mesh,
        in_specs=placed,
        out_specs=(P(("dp", "tensor"), None), P("dp", None, "tensor")),
        check_vma=False,
    )
```

time: 499 us -> 93.6 us (0.19); the launches traced: 493 us -> 93.3 us
  waiting for transfers between devices: 244 us -> 0 us
  local copies, waits for them, and re-layouts: 182 us -> 8.58 us
  Pallas kernels: 0 us -> 84 us
  other arithmetic: 26.6 us -> 0 us
  matrix products: 23.4 us -> 0 us
  between operations: 15.3 us -> 0.65 us
    reduce_scatter x1 -> x0, waiting for transfers between devices: 216 us -> none  [local(): lax.psum_scatter(jnp.dot(flat_spread, out_weight, preferred_element_type=...]
    scatter x9 -> x0, local copies, waits for them, and re-layouts: 96.6 us -> none  [the longest x4 78.4 us: local(): spread = spread.at[target, :, expert_slot].set(gated, mode='drop')]
    pallas_call x0 -> x1, Pallas kernels: none -> 84 us  [local(): pl.pallas_call(layer, out_shape=(jax.ShapeDtypeStruct(hidden.shape, jnp.b...]
    gather x21 -> x0, local copies, waits for them, and re-layouts: 75.1 us -> none  [the longest x4 31.1 us: local(): normed[slot_tok]]
    all_gather x1 -> x0, waiting for transfers between devices: 28.1 us -> none  [local(): lax.all_gather(normalize(hidden, norm_gain), 'tensor', axis=0, tiled=True)]
    dot_general x15 -> x0, matrix products: 23.4 us -> none  [the longest x4 9.93 us: local(): jnp.einsum('cd,dhk->chk', normed[slot_tok], query_cols[:, :, expert_slot]...]
    concatenate x11 -> x0, other arithmetic: 10.4 us -> none  [the longest x4 4.88 us: local(): gate_here = gates[slot_tok, expert] * is_valid.astype(jnp.float32)]
    convert_element_type x13 -> x0, other arithmetic: 7.31 us -> none  [the longest x5 2.44 us: rotate(): angles = positions.astype(jnp.float32)[:, None] * frequency[None, :]]
  transfers between devices with their start and end apart: 3 -> 0, of which waited for: 2 -> 0; matrix products, arithmetic and copies ran while one was open for 22% -> 0% of each run, Pallas kernels for 0% -> 0%
where the time goes in v1:
time: 93.6 us; the launch traced here: 93.3 us
  Pallas kernels  84 us (90%)
  local copies, waits for them, and re-layouts  8.58 us (9%)
    pallas_call x1, Pallas kernels, local(): pl.pallas_call(layer, out_shape=(jax.ShapeDtypeStruct(hidden.shape, jnp.b...  84 us
    unnamed x18, local copies, waits for them, and re-layouts  7.89 us

profile of v1, /device:TPU:8, one launch (start us, length us, event | category | flops | bytes accessed | tf_op | source)
XLA Modules:
  0.0 93.3 jit_solution(1675836920099201409)
XLA Ops:
  0.6 0.7 reshape.10.gain
  1.3 0.0 copy-start
  1.3 1.0 %copy-done = bf16[2048,128]{1,0:T(8,128)(2,1)S(1)} copy-done((bf16[2048,128]{1,0:T(8,128)(2,1)S(1)}, bf16[2048,128]{1,0:T(8,128)(2,1)}, u32[]{:S(2)}) %copy-start) | copy-done | bytes 524312
  2.4 0.0 copy-start.1
  2.4 1.0 %copy-done.1 = bf16[16,128,128]{2,1,0:T(8,128)(2,1)S(1)} copy-done((bf16[16,128,128]{2,1,0:T(8,128)(2,1)S(1)}, bf16[16,128,128]{2,1,0:T(8,128)(2,1)}, u32[]{:S(2)}) %copy-start.1) | copy-done | bytes 524312
  3.4 0.0 copy-start.2
  3.4 0.9 copy-done.2
  4.3 0.0 copy-start.3
  4.3 0.8 copy-done.3
  5.1 0.0 copy-start.4
  5.1 0.7 copy-done.4
  5.8 0.0 copy-start.5
  5.8 0.7 copy-done.5
  6.5 0.0 copy-start.6
  6.5 0.7 copy-done.6
  7.1 0.0 copy-start.7
  7.1 0.7 copy-done.7
  7.8 84.0 %layer.1 = (bf16[32,2048]{1,0:T(8,128)(2,1)S(1)}, bf16[16,128,128]{2,1,0:T(8,128)(2,1)S(1)}) custom-call(bf16[32,2048]{1,0:T(8,128)(2,1)S(1)} %copy-done.2, bf16[1,2048]{1,0:T(2,128)(2,1)S(1)} %reshape.10.gain, bf16[8,2048]{1,0:T(8,128)(2,1)S(1)} %bitcast.3, bf16[2048,128]{1,0:T(8,128)(2,1)S(1)} %copy-done, bf16[2048,512]{1,0:T(8,128)(2,1)} %query_weight.1, ...), custom_call_target="tpu_custom_call" | custom-call | tf_op jit(solution)/shard_map/layer/pallas_call | solution.py:374
  91.8 0.7 copy.15
  92.5 0.8 copy.16
Async XLA Ops:
  1.3 1.0 %copy-start = (bf16[2048,128]{1,0:T(8,128)(2,1)S(1)}, bf16[2048,128]{1,0:T(8,128)(2,1)}, u32[]{:S(2)}) copy-start(bf16[2048,128]{1,0:T(8,128)(2,1)} %kv_weight.1) | copy-start | bytes 1572868
  2.4 1.0 %copy-start.1 = (bf16[16,128,128]{2,1,0:T(8,128)(2,1)S(1)}, bf16[16,128,128]{2,1,0:T(8,128)(2,1)}, u32[]{:S(2)}) copy-start(bf16[16,128,128]{2,1,0:T(8,128)(2,1)} %cache.1) | copy-start | bytes 1572868
  3.4 0.9 copy-start.2
  4.3 0.8 copy-start.3
  5.1 0.7 copy-start.4
  5.8 0.7 copy-start.5
  6.5 0.7 copy-start.6
  7.1 0.7 copy-start.7

commit v2 on v1

--- a/solution.py
+++ b/solution.py
@@ -10,10 +10,11 @@
 
 NX, NZ, ROWS, D, HD = 4, 8, 32, 2048, 128
 EXPERTS = 4
-HALF = ROWS // 2
+GATHER_CUT, REDUCE_CUT = 768, 896
 X_OFFSETS = (0, -1, 1, -2)
 Z_OFFSETS = (0, -1, 1, -2, 2, -3, 3, -4)
-SEND_US, LATENCY_US = 1.31, 1.0
+GROUPS = ((0,), (-1, 1), (-2, 2), (-3, 3), (-4,))
+LINK_BYTES_PER_US, LATENCY_US = 86600.0, 2.3
 
 
 def gather_tasks():
@@ -89,12 +90,12 @@
 
 
 def compute_tasks():
-    tasks = [dict(name=("norm",), after=[], cost=1.0)]
-    tasks += [dict(name=("setup", n), after=[], cost=1.0) for n in range(4)]
-    for j in Z_OFFSETS:
-        after = [("recv", half, i, j) for half in "AB" for i in X_OFFSETS] + [("setup", n) for n in range(4)]
-        tasks.append(dict(name=("project", j), after=after, cost=0.9))
-    everything = [("project", j) for j in Z_OFFSETS]
+    tasks = [dict(name=("norm",), after=[], cost=2.0)]
+    tasks += [dict(name=("setup", n), after=[], cost=0.8) for n in range(4)]
+    for group in GROUPS:
+        after = [("recv", half, i, j) for half in "AB" for i in X_OFFSETS for j in group] + [("setup", n) for n in range(4)]
+        tasks.append(dict(name=("project", *group), after=after, cost=0.1 + 0.7 * len(group)))
+    everything = [("project", *group) for group in GROUPS]
     tasks.append(dict(name=("swap",), after=everything, cost=1.5))
     for i in (2, -1, 1, 0):
         tasks.append(dict(name=("attend", i), after=[("swap",)], cost=2.0))
@@ -124,23 +125,28 @@
             work.remove(task)
         clock += task["cost"]
         for link, key in task.get("sends", []):
-            begin = max(clock, free.get(link, 0.0))
-            free[link] = begin + SEND_US
-            arrived[key] = begin + SEND_US + LATENCY_US
+            cut = GATHER_CUT if len(key) == 3 and not isinstance(key[1], str) else REDUCE_CUT
+            columns = cut if key[0] == "A" else D - cut
+            free[link[0]] = max(clock, free.get(link[0], 0.0)) + ROWS * columns * 2 / LINK_BYTES_PER_US
+            arrived[key] = free[link[0]] + LATENCY_US
         done.add(task["name"])
         order.append(task)
     return order, clock
 
 
+FREQUENCY = [float(f) for f in (10000.0 ** (-np.arange(64, dtype=np.float32) / np.float32(64))).astype(np.float32)]
 GATHER_KEYS = [t["block"] for t in gather_tasks() if t["deps"]]
 REDUCE_KEYS = [key for t in reduce_tasks() for _, key in t["sends"]]
+REDUCE_KEYS.sort(key=lambda key: key[0])
+A_SLOTS = sum(key[0] == "A" for key in REDUCE_KEYS)
 
 
 def layer(
-    hidden, gain, router, kv_weight, query_weight, out_weight, routes, segments, frequency, pages, cache,
-    out, new_cache,
-    full, part, landed, weight, out_w, pool, kv, query, cosine, sine, route, gate, mixed,
-    gather_send, gather_recv, reduce_send, reduce_recv, kv_send, kv_recv, load, store,
+    hidden_at, gain_at, router_at, kv_weight, query_weight, out_weight, routes_at, segments_at, pages_at, cache,
+    out, pool,
+    hidden, gain, router, routes, segments, pages,
+    full, part, landed_a, landed_b, weight, out_w, kv, query, cosine, sine, route, gate, mixed,
+    gather_send, gather_recv, reduce_send, reduce_recv, kv_send, kv_recv, load,
 ):
     me = lax.axis_index("tensor")
     turn = 1 - 2 * lax.rem(lax.axis_index("dp"), 2)
@@ -166,6 +172,14 @@
     for device in links.values():
         pl.semaphore_signal(barrier, inc=1, device_id={"tensor": device}, device_id_type=pl.DeviceIdType.MESH)
 
+    early = [
+        pltpu.make_async_copy(src, dst, load.at[4 + n])
+        for n, (src, dst) in enumerate(
+            [(hidden_at, hidden), (gain_at, gain), (router_at, router), (routes_at, routes), (segments_at, segments), (pages_at, pages)]
+        )
+    ]
+    for copy in early:
+        copy.start()
     loads = [
         pltpu.make_async_copy(query_weight, weight.at[:, 0:512], load.at[0]),
         pltpu.make_async_copy(kv_weight, weight.at[:, 512:640], load.at[1]),
@@ -175,8 +189,8 @@
     for copy in loads:
         copy.start()
 
-    def rows_of(half):
-        return pl.ds(0 if half == "A" else HALF, HALF)
+    def columns_of(half, cut):
+        return pl.ds(0, cut) if half == "A" else pl.ds(cut, D - cut)
 
     def remote(src, dst, send, recv, device):
         return pltpu.make_async_remote_copy(
@@ -190,13 +204,24 @@
     waiting = []
 
     def norm():
+        for copy in early[:2]:
+            copy.wait()
         values = hidden[...].astype(jnp.float32)
         factor = lax.rsqrt(jnp.mean(values * values, axis=-1, keepdims=True) + 1e-05)
-        full[z, x] = (values * factor * gain[...].astype(jnp.float32)).astype(jnp.bfloat16)
+        gains = gain[...].astype(jnp.float32)
+        for c in range(D // 128):
+            at = slice(c * 128, c * 128 + 128)
+            full[z, x, :, at] = (values[:, at] * factor * gains[c : c + 1]).astype(jnp.bfloat16)
         pl.semaphore_wait(barrier, 4)
 
     def setup(n):
+        if n == 0:
+            for copy in early[2:]:
+                copy.wait()
         seg = segments[...]
+        frequency = jnp.zeros((1, 128), jnp.float32)
+        for f, value in enumerate(FREQUENCY):
+            frequency = jnp.where(lax.rem(lane[0:1], HD // 2) == f, value, frequency)
         starts = [jnp.sum((seg < s).astype(jnp.float32), axis=1, keepdims=True) for s in (1, 2, 3)]
         for b in (2 * n, 2 * n + 1):
             token = (sub + b * 128).astype(jnp.float32)
@@ -208,7 +233,7 @@
             columns = jnp.where(sub == 0, first, jnp.where(sub == 1, second, 0.0)).T
             at = (b // 2, pl.ds(b % 2 * 4, 4))
             route[at] = jnp.where(lane == 2, start, columns).reshape(4, 32, 128)
-            angle = (token - start) * frequency[...]
+            angle = (token - start) * frequency
             k = jnp.floor(angle * 0.6366197723675814 + 0.5)
             r = angle - k * 1.5703125
             r = r - k * 4.837512969970703e-4
@@ -237,10 +262,16 @@
     def rotate(values, c, s):
         return values * c + pltpu.roll(values, HD // 2, 1) * s
 
-    def project(j):
+    def project(*group):
+        rows = [full[fz(j)].reshape(128, D) for j in group]
+        rows = rows[0] if len(group) == 1 else jnp.concatenate(rows, axis=0)
+        made = jnp.dot(rows, weight[...], preferred_element_type=jnp.float32)
+        for n, j in enumerate(group):
+            place(j, made[n * 128 : n * 128 + 128])
+
+    def place(j, made):
         za = fz(j)
         at = (slice(None), pl.ds(za, 1))
-        made = jnp.dot(full[za].reshape(128, D), weight[...], preferred_element_type=jnp.float32)
         picks = route[at].reshape(128, 128)
         c, s = cosine[at].reshape(128, 128), sine[at].reshape(128, 128)
         for n in range(2):
@@ -261,8 +292,8 @@
         first, second = jnp.exp(first - top), jnp.exp(second - top)
         total = first + second
         gate[at] = jnp.where(lane == 0, first / total, second / total).reshape(4, 1, 32, 128)
-        place = kv.at[parity, 2:6, za]
-        copy = remote(place, place, kv_send.at[j % NZ], kv_recv.at[j % NZ], partner)
+        rows = kv.at[parity, 2:6, za]
+        copy = remote(rows, rows, kv_send.at[j % NZ], kv_recv.at[j % NZ], partner)
         copy.start()
         waiting.append(copy)
 
@@ -311,13 +342,10 @@
             return 0
 
         lax.fori_loop(0, 16, page, 0)
-        copy = pltpu.make_async_copy(pool, new_cache, store)
-        copy.start()
-        return copy
 
     def receive(task):
         half, i, j = task["block"]
-        place = full.at[fz(j), fx(i), rows_of(half)]
+        place = full.at[fz(j), fx(i), :, columns_of(half, GATHER_CUT)]
         if task["deps"]:
             n = GATHER_KEYS.index(task["deps"][0])
             remote(place, place, gather_send.at[n], gather_recv.at[n], me).wait_recv()
@@ -329,26 +357,30 @@
 
     def combine(task):
         half, i, j = task["block"]
-        at = (fx(i), fz(j), rows_of(half))
+        columns = columns_of(half, REDUCE_CUT)
+        at = (fx(i), fz(j), slice(None), columns)
+
+        def landed(n):
+            return landed_a.at[n] if half == "A" else landed_b.at[n - A_SLOTS]
+
         slots = [REDUCE_KEYS.index(key) for key in task["deps"]]
         for n in slots:
-            remote(landed.at[n], landed.at[n], reduce_send.at[n], reduce_recv.at[n], me).wait_recv()
+            remote(landed(n), landed(n), reduce_send.at[n], reduce_recv.at[n], me).wait_recv()
         if slots:
             total = part[at].astype(jnp.float32)
             for n in slots:
-                total = total + landed[n].astype(jnp.float32)
+                total = total + landed(n)[...].astype(jnp.float32)
             if not task["sends"]:
-                total = total + hidden[rows_of(half), :].astype(jnp.float32)
-                out[rows_of(half), :] = total.astype(jnp.bfloat16)
+                total = total + hidden[:, columns].astype(jnp.float32)
+                out[:, columns] = total.astype(jnp.bfloat16)
             else:
                 part[at] = total.astype(jnp.bfloat16)
         for link, key in task["sends"]:
             n = REDUCE_KEYS.index(key)
-            copy = remote(part.at[at], landed.at[n], reduce_send.at[n], reduce_recv.at[n], links[link])
+            copy = remote(part.at[at], landed(n), reduce_send.at[n], reduce_recv.at[n], links[link])
             copy.start()
             waiting.append(copy)
 
-    stored = None
     for task in plan()[0]:
         kind, *rest = task["name"]
         if kind == "recv":
@@ -356,20 +388,15 @@
         elif kind == "sum":
             combine(task)
         elif kind == "cache":
-            stored = update_cache()
+            update_cache()
         else:
             dict(norm=norm, setup=setup, project=project, swap=swap, attend=attend)[kind](*rest)
     for copy in waiting:
         copy.wait_send()
-    stored.wait()
 
 
 def local(hidden, gain, router, kv_weight, query_weight, out_weight, routes, segments, pages, cache):
-    half = HD // 2
-    frequency = (10000.0 ** (-np.arange(half, dtype=np.float32) / np.float32(half))).astype(np.float32)
-    frequency = np.concatenate([frequency, frequency])[None]
-    vmem = pl.BlockSpec(memory_space=pltpu.VMEM)
-    anywhere = pl.BlockSpec(memory_space=pl.ANY)
+    vmem, hbm = pl.BlockSpec(memory_space=pltpu.VMEM), pl.BlockSpec(memory_space=pltpu.HBM)
     dma = pltpu.SemaphoreType.DMA
     return pl.pallas_call(
         layer,
@@ -377,15 +404,21 @@
             jax.ShapeDtypeStruct(hidden.shape, jnp.bfloat16),
             jax.ShapeDtypeStruct(cache.shape, jnp.bfloat16),
         ),
-        in_specs=[vmem] * 3 + [anywhere] * 3 + [vmem] * 3 + [pl.BlockSpec(memory_space=pltpu.SMEM), anywhere],
-        out_specs=(vmem, anywhere),
+        in_specs=[hbm] * 10,
+        out_specs=(vmem, vmem),
         scratch_shapes=[
+            pltpu.VMEM((ROWS, D), jnp.bfloat16),
+            pltpu.VMEM((D // 128, 128), jnp.bfloat16),
+            pltpu.VMEM((8, D), jnp.bfloat16),
+            pltpu.VMEM((2, 1024), jnp.int32),
+            pltpu.VMEM((1, 1024), jnp.int32),
+            pltpu.SMEM((8,), jnp.int32),
             pltpu.VMEM((NZ, NX, ROWS, D), jnp.bfloat16),
             pltpu.VMEM((NX, NZ, ROWS, D), jnp.bfloat16),
-            pltpu.VMEM((len(REDUCE_KEYS), HALF, D), jnp.bfloat16),
+            pltpu.VMEM((A_SLOTS, ROWS, REDUCE_CUT), jnp.bfloat16),
+            pltpu.VMEM((len(REDUCE_KEYS) - A_SLOTS, ROWS, D - REDUCE_CUT), jnp.bfloat16),
             pltpu.VMEM((D, 768), jnp.bfloat16),
             pltpu.VMEM((512, D), jnp.bfloat16),
-            pltpu.VMEM((16, 128, HD), jnp.bfloat16),
             pltpu.VMEM((2, NX + 2, NZ, ROWS, HD), jnp.bfloat16),
             pltpu.VMEM((2, NX, NZ, ROWS, HD), jnp.bfloat16),
             pltpu.VMEM((NX, NZ, ROWS, HD), jnp.float32),
@@ -399,16 +432,15 @@
             dma((len(REDUCE_KEYS),)),
             dma((NZ,)),
             dma((NZ,)),
-            dma((4,)),
-            dma(()),
+            dma((10,)),
         ],
         compiler_params=pltpu.CompilerParams(
-            collective_id=0, has_side_effects=True, vmem_limit_bytes=52 * 1024 * 1024
+            collective_id=0, has_side_effects=True, vmem_limit_bytes=63 * 1024 * 1024
         ),
         name="layer",
     )(
-        hidden, gain.reshape(1, D), router.T, kv_weight, query_weight, out_weight, routes.T,
-        segments.reshape(1, -1), jnp.asarray(frequency), pages, cache,
+        hidden, gain.reshape(D // 128, 128), router.T, kv_weight, query_weight, out_weight, routes.T,
+        segments.reshape(1, -1), pages, cache,
     )
 
 

time: 93.6 us -> 84.9 us (0.907)
  local copies, waits for them, and re-layouts: 8.58 us -> 3.45 us
  Pallas kernels: 84 us -> 80.6 us
    unnamed x18 -> x2, local copies, waits for them, and re-layouts: 7.89 us -> 3.45 us
    pallas_call x1, Pallas kernels: 84 us -> 80.6 us  [local(): pl.pallas_call(layer, out_shape=(jax.ShapeDtypeStruct(hidden.shape, jnp.b...]
where the time goes in v2:
time: 84.9 us; the launch traced here: 84.7 us
  Pallas kernels  80.6 us (95%)
  local copies, waits for them, and re-layouts  3.45 us (4%)
    pallas_call x1, Pallas kernels, local(): pl.pallas_call(layer, out_shape=(jax.ShapeDtypeStruct(hidden.shape, jnp.b...  80.6 us
    unnamed x2, local copies, waits for them, and re-layouts  3.45 us

profile of v2, /device:TPU:8, one launch (start us, length us, event | category | flops | bytes accessed | tf_op | source)
XLA Modules:
  0.0 84.7 jit_solution(8004745249167341005)
XLA Ops:
  0.6 80.6 %layer.1 = (bf16[32,2048]{1,0:T(8,128)(2,1)}, bf16[16,128,128]{2,1,0:T(8,128)(2,1)}) custom-call(bf16[32,2048]{1,0:T(8,128)(2,1)} %hidden_at.1, bf16[16,128]{1,0:T(8,128)(2,1)} %bitcast.6, bf16[8,2048]{1,0:T(8,128)(2,1)} %bitcast.4, bf16[2048,128]{1,0:T(8,128)(2,1)} %kv_weight.1, bf16[2048,512]{1,0:T(8,128)(2,1)} %query_weight.1, ...), custom_call_target="tpu_custom_call" | custom-call | tf_op jit(solution)/shard_map/layer/pallas_call | solution.py:401
  81.3 1.6 %copy.14 = bf16[32,2048]{1,0:T(8,128)(2,1)} copy(bf16[32,2048]{1,0:T(8,128)(2,1)} %get-tuple-element.4) | data formatting | bytes 262144
  82.9 1.9 %copy.15 = bf16[16,128,128]{2,1,0:T(8,128)(2,1)} copy(bf16[16,128,128]{2,1,0:T(8,128)(2,1)} %get-tuple-element.5) | data formatting | bytes 1048576

commit v3 on v2

--- a/solution.py
+++ b/solution.py
@@ -11,101 +11,96 @@
 NX, NZ, ROWS, D, HD = 4, 8, 32, 2048, 128
 EXPERTS = 4
 GATHER_CUT, REDUCE_CUT = 768, 896
-X_OFFSETS = (0, -1, 1, -2)
-Z_OFFSETS = (0, -1, 1, -2, 2, -3, 3, -4)
-GROUPS = ((0,), (-1, 1), (-2, 2), (-3, 3), (-4,))
-LINK_BYTES_PER_US, LATENCY_US = 86600.0, 2.3
-
-
-def gather_tasks():
+Z_OFFSETS = (0, 1, 7, 2, 6, 3, 5, 4)
+GROUPS = ((0,), (1, 7), (2, 6), (3, 5), (4,))
+ATTEND_ORDER = (2, 1, 3, 0)
+GATHER_CUT, REDUCE_CUT = 768, 896
+LINK_BYTES_PER_US, LATENCY_US = 43000.0, 2.1
+FREQUENCY = [float(f) for f in (10000.0 ** (-np.arange(64, dtype=np.float32) / np.float32(64))).astype(np.float32)]
+
+RING4 = {0: (1, -1), 1: (2,)}
+CHAIN8 = {0: (1, -1), 1: (2,), 2: (3,), 3: (4,), -1: (-2,), -2: (-3,)}
+SKIP8 = {0: (1, 2, -1), 2: (3,), 3: (4,), -1: (-2,), -2: (-3,)}
+WIDE8 = {0: (1, -1, 2, -2), 2: (3, 4), -2: (-3,)}
+
+
+def turned(tree, n, sign):
+    return {sign * p % n: tuple(sign * q % n for q in rest) for p, rest in tree.items()}
+
+
+def x_tree(half, pz):
+    return turned(RING4, NX, 1 if half == "A" or pz % 2 else -1)
+
+
+def z_tree(phase, half, px):
+    if half == "A":
+        return turned(CHAIN8, NZ, 1 if px < 2 else -1)
+    return turned(SKIP8 if phase == "gather" else WIDE8, NZ, -1)
+
+
+def children(phase, half, px, pz):
+    found = []
+    if half == "B" or pz == 0:
+        found += [(q, pz) for q in x_tree(half, pz).get(px, ())]
+    if half == "A" or px == 0:
+        found += [(px, q) for q in z_tree(phase, half, px).get(pz, ())]
+    return found
+
+
+def parent(phase, half, px, pz):
+    places = [(i, j) for i in range(NX) for j in range(NZ)]
+    return next((p for p in places if (px, pz) in children(phase, half, *p)), None)
+
+
+def links_of(one, other):
+    dx, dz = (other[0] - one[0]) % NX, (other[1] - one[1]) % NZ
+    if dx:
+        return ("x+", 1) if dx == 1 else ("x-", 1)
+    return ("z+", dz) if dz < 4 else ("z-", NZ - dz)
+
+
+def move_tasks():
     tasks = []
     for half in "AB":
-        for i in X_OFFSETS:
-            for j in Z_OFFSETS:
-                sends = []
-                if half == "A":
-                    if j == 0 and i in (0, -1):
-                        sends.append(("x+", (half, i - 1, 0)))
-                    if j == 0 and i == 0:
-                        sends.append(("x-", (half, 1, 0)))
-                if -4 < j <= 0 and (half == "A" or i == 0):
-                    sends.append(("z+", (half, i, j - 1)))
-                if 0 <= j < 3 and (half == "A" or i == 0):
-                    sends.append(("z-", (half, i, j + 1)))
-                if half == "B":
-                    if i in (0, -1):
-                        sends.append(("x+", (half, i - 1, j)))
-                    if i == 0:
-                        sends.append(("x-", (half, 1, j)))
-                own = i == 0 and j == 0
-                tasks.append(
-                    dict(
-                        name=("recv", half, i, j),
-                        deps=[] if own else [(half, i, j)],
-                        after=[("norm",)] if own else [],
-                        sends=sends,
-                        block=(half, i, j),
-                        cost=0.05,
-                    )
-                )
-    return tasks
-
-
-def reduce_tasks():
-    tasks = []
-
-    def add(half, i, j, deps, sends, cost):
-        tasks.append(
-            dict(name=("sum", half, i, j, len(tasks)), deps=deps, after=[("attend", i)], sends=sends, block=(half, i, j), cost=cost)
-        )
-
-    for i in (2, -1, 1, 0):
-        for k in (4, 3, 2, 1):
-            add("A", i, k, [("A", "L", i, k)] if k < 4 else [], [("z+", ("A", "L", i, k - 1))], 0.1)
-        for k in (-3, -2, -1):
-            add("A", i, k, [("A", "S", i, k)] if k > -3 else [], [("z-", ("A", "S", i, k + 1))], 0.1)
-        deps = [("A", "L", i, 0), ("A", "S", i, 0)]
-        if i == 1:
-            deps.append(("A", "X", 1))
-        if i == 0:
-            deps += [("A", "X", 0), ("A", "Y", 0)]
-        sends = {2: [("x+", ("A", "X", 1))], -1: [("x-", ("A", "Y", 0))], 1: [("x+", ("A", "X", 0))], 0: []}[i]
-        add("A", i, 0, deps, sends, 0.15)
-    for j in (4, -3, 3, -2, 2, -1, 1, 0):
-        add("B", 2, j, [], [("x+", ("B", "L", 1, j))], 0.1)
-        add("B", -1, j, [], [("x-", ("B", "S", 0, j))], 0.1)
-        add("B", 1, j, [("B", "L", 1, j)], [("x+", ("B", "L", 0, j))], 0.1)
-        deps = [("B", "L", 0, j), ("B", "S", 0, j)]
-        sends = []
-        if j > 0:
-            deps += [("B", "Z", j)] if j < 4 else []
-            sends = [("z+", ("B", "Z", j - 1))]
-        elif j < 0:
-            deps += [("B", "W", j)] if j > -3 else []
-            sends = [("z-", ("B", "W", j + 1))]
-        else:
-            deps += [("B", "Z", 0), ("B", "W", 0)]
-        add("B", 0, j, deps, sends, 0.15)
+        for px in range(NX):
+            for pz in range(NZ):
+                own = (px, pz) == (0, 0)
+                here = ("gather", half, px, pz)
+                sends = [((px, pz), q, ("gather", half, *q)) for q in children(*here)]
+                tasks.append(dict(name=here, deps=[] if own else [here], after=[("norm",)] if own else [], sends=sends, cost=0.06))
+    for half in "AB":
+        for px in ATTEND_ORDER:
+            for pz in range(NZ):
+                here = ("reduce", half, px, pz)
+                deps = [("reduce", half, *q) for q in children(*here)]
+                up = parent(*here)
+                sends = [((px, pz), up, here)] if up else []
+                tasks.append(dict(name=here, deps=deps, after=[("attend", px)], sends=sends, cost=0.06))
     return tasks
 
 
 def compute_tasks():
     tasks = [dict(name=("norm",), after=[], cost=2.0)]
-    tasks += [dict(name=("setup", n), after=[], cost=0.8) for n in range(4)]
+    tasks += [dict(name=("setup", n), after=[], cost=0.6) for n in range(4)]
     for group in GROUPS:
-        after = [("recv", half, i, j) for half in "AB" for i in X_OFFSETS for j in group] + [("setup", n) for n in range(4)]
-        tasks.append(dict(name=("project", *group), after=after, cost=0.1 + 0.7 * len(group)))
+        after = [("gather", half, i, j) for half in "AB" for i in range(NX) for j in group] + [("setup", n) for n in range(4)]
+        tasks.append(dict(name=("project", *group), after=after, cost=0.25 + 0.75 * len(group)))
     everything = [("project", *group) for group in GROUPS]
-    tasks.append(dict(name=("swap",), after=everything, cost=1.5))
-    for i in (2, -1, 1, 0):
-        tasks.append(dict(name=("attend", i), after=[("swap",)], cost=2.0))
-    tasks.append(dict(name=("cache",), after=[("swap",), ("attend", 0)], cost=1.0))
+    tasks.append(dict(name=("swap",), after=everything, cost=2.5))
+    for i in ATTEND_ORDER:
+        tasks.append(dict(name=("attend", i), after=[("swap",)], cost=1.75))
+    tasks.append(dict(name=("cache",), after=[("swap",), ("attend", ATTEND_ORDER[-1])], cost=1.0))
     return tasks
+
+
+def columns_in(phase, half):
+    cut = GATHER_CUT if phase == "gather" else REDUCE_CUT
+    return (0, cut) if half == "A" else (cut, D - cut)
 
 
 @functools.cache
 def plan():
-    moves, work = gather_tasks() + reduce_tasks(), compute_tasks()
+    moves, work = move_tasks(), compute_tasks()
     clock, done, arrived, free, order = 0.0, set(), {}, {}, []
     while moves or work:
         best = None
@@ -114,9 +109,8 @@
                 at = max([arrived[d] for d in task["deps"]], default=0.0)
                 if best is None or at < best[0]:
                     best = (at, task)
-        ready = best is not None and best[0] <= clock
         task = None
-        if not ready:
+        if best is None or best[0] > clock:
             task = next((w for w in work if all(a in done for a in w["after"])), None)
         if task is None:
             clock, task = max(clock, best[0]), best[1]
@@ -124,21 +118,21 @@
         else:
             work.remove(task)
         clock += task["cost"]
-        for link, key in task.get("sends", []):
-            cut = GATHER_CUT if len(key) == 3 and not isinstance(key[1], str) else REDUCE_CUT
-            columns = cut if key[0] == "A" else D - cut
-            free[link[0]] = max(clock, free.get(link[0], 0.0)) + ROWS * columns * 2 / LINK_BYTES_PER_US
-            arrived[key] = free[link[0]] + LATENCY_US
+        for one, other, key in task.get("sends", []):
+            link, hops = links_of(one, other)
+            took = ROWS * columns_in(*key[:2])[1] * 2 / LINK_BYTES_PER_US
+            free[link] = max(clock, free.get(link, 0.0)) + took * hops
+            arrived[key] = free[link] - took * (hops - 1) + LATENCY_US
         done.add(task["name"])
         order.append(task)
     return order, clock
 
 
-FREQUENCY = [float(f) for f in (10000.0 ** (-np.arange(64, dtype=np.float32) / np.float32(64))).astype(np.float32)]
-GATHER_KEYS = [t["block"] for t in gather_tasks() if t["deps"]]
-REDUCE_KEYS = [key for t in reduce_tasks() for _, key in t["sends"]]
-REDUCE_KEYS.sort(key=lambda key: key[0])
-A_SLOTS = sum(key[0] == "A" for key in REDUCE_KEYS)
+def slot(half, px, pz):
+    return px * NZ + pz - 1
+
+
+SLOTS = NX * NZ - 1
 
 
 def layer(
@@ -154,22 +148,20 @@
     parity = lax.rem(z, 2)
     base = parity * EXPERTS
 
-    def fx(i):
-        return lax.rem(x + turn * i + NX, NX)
-
-    def fz(j):
-        return lax.rem(z + turn * j + NZ, NZ)
-
-    links = {
-        "x+": fx(1) * NZ + z,
-        "x-": fx(-1) * NZ + z,
-        "z+": x * NZ + fz(1),
-        "z-": x * NZ + fz(-1),
-    }
+    def fx(px):
+        return lax.rem(x - turn * px + 2 * NX, NX)
+
+    def fz(pz):
+        return lax.rem(z - turn * pz + 2 * NZ, NZ)
+
+    def device_at(one, other):
+        return fx(one[0] - other[0]) * NZ + fz(one[1] - other[1])
+
+    near = [device_at((0, 0), p) for p in ((1, 0), (-1, 0), (0, 1), (0, -1), (0, 2), (0, -2))]
     partner = x * NZ + z + 1 - 2 * parity
 
     barrier = pltpu.get_barrier_semaphore()
-    for device in links.values():
+    for device in near:
         pl.semaphore_signal(barrier, inc=1, device_id={"tensor": device}, device_id_type=pl.DeviceIdType.MESH)
 
     early = [
@@ -189,8 +181,8 @@
     for copy in loads:
         copy.start()
 
-    def columns_of(half, cut):
-        return pl.ds(0, cut) if half == "A" else pl.ds(cut, D - cut)
+    def columns_of(phase, half):
+        return pl.ds(*columns_in(phase, half))
 
     def remote(src, dst, send, recv, device):
         return pltpu.make_async_remote_copy(
@@ -212,7 +204,7 @@
         for c in range(D // 128):
             at = slice(c * 128, c * 128 + 128)
             full[z, x, :, at] = (values[:, at] * factor * gains[c : c + 1]).astype(jnp.bfloat16)
-        pl.semaphore_wait(barrier, 4)
+        pl.semaphore_wait(barrier, len(near))
 
     def setup(n):
         if n == 0:
@@ -265,11 +257,14 @@
     def project(*group):
         rows = [full[fz(j)].reshape(128, D) for j in group]
         rows = rows[0] if len(group) == 1 else jnp.concatenate(rows, axis=0)
-        made = jnp.dot(rows, weight[...], preferred_element_type=jnp.float32)
+        made = jnp.dot(rows, weight[:, 512:768], preferred_element_type=jnp.float32)
         for n, j in enumerate(group):
-            place(j, made[n * 128 : n * 128 + 128])
-
-    def place(j, made):
+            place_kv(j, made[n * 128 : n * 128 + 128])
+        made = jnp.dot(rows, weight[:, 0:512], preferred_element_type=jnp.float32)
+        for n, j in enumerate(group):
+            place_queries(j, made[n * 128 : n * 128 + 128])
+
+    def place_queries(j, made):
         za = fz(j)
         at = (slice(None), pl.ds(za, 1))
         picks = route[at].reshape(128, 128)
@@ -281,10 +276,20 @@
                 values = jnp.where(local == float(e), made[:, e * HD : e * HD + HD], values)
             values = rotate(values, c, s) * (HD**-0.5)
             query[(n, *at)] = values.astype(jnp.bfloat16).reshape(4, 1, 32, 128)
-        own = made[:, 512:640]
+
+    def place_kv(j, made):
+        za = fz(j)
+        at = (slice(None), pl.ds(za, 1))
+        picks = route[at].reshape(128, 128)
+        c, s = cosine[at].reshape(128, 128), sine[at].reshape(128, 128)
+        own = made[:, 0:128]
         own = jnp.where(parity == 0, rotate(own, c, s), own)
         kv[parity, 2:6, pl.ds(za, 1)] = own.astype(jnp.bfloat16).reshape(4, 1, 32, 128)
-        logits = made[:, 640:768]
+        rows = kv.at[parity, 2:6, za]
+        copy = remote(rows, rows, kv_send.at[j], kv_recv.at[j], partner)
+        copy.start()
+        waiting.append(copy)
+        logits = made[:, 128:256]
         lanes = lane.astype(jnp.float32)
         first = jnp.sum(jnp.where(lanes == picks[:, 0:1], logits, 0.0), axis=1, keepdims=True)
         second = jnp.sum(jnp.where(lanes == picks[:, 1:2], logits, 0.0), axis=1, keepdims=True)
@@ -292,16 +297,12 @@
         first, second = jnp.exp(first - top), jnp.exp(second - top)
         total = first + second
         gate[at] = jnp.where(lane == 0, first / total, second / total).reshape(4, 1, 32, 128)
-        rows = kv.at[parity, 2:6, za]
-        copy = remote(rows, rows, kv_send.at[j % NZ], kv_recv.at[j % NZ], partner)
-        copy.start()
-        waiting.append(copy)
 
     def swap():
         for j in Z_OFFSETS:
-            zp = lax.rem(z + 1 - 2 * parity + turn * j + NZ, NZ)
+            zp = lax.rem(z + 1 - 2 * parity - turn * j + 2 * NZ, NZ)
             place = kv.at[1 - parity, 2:6, zp]
-            remote(place, place, kv_send.at[j % NZ], kv_recv.at[j % NZ], partner).wait_recv()
+            remote(place, place, kv_send.at[j], kv_recv.at[j], partner).wait_recv()
 
     def attend(i):
         xa = fx(i)
@@ -343,50 +344,45 @@
 
         lax.fori_loop(0, 16, page, 0)
 
-    def receive(task):
-        half, i, j = task["block"]
-        place = full.at[fz(j), fx(i), :, columns_of(half, GATHER_CUT)]
+    def receive(half, px, pz, task):
+        block = full.at[fz(pz), fx(px), :, columns_of("gather", half)]
         if task["deps"]:
-            n = GATHER_KEYS.index(task["deps"][0])
-            remote(place, place, gather_send.at[n], gather_recv.at[n], me).wait_recv()
-        for link, key in task["sends"]:
-            n = GATHER_KEYS.index(key)
-            copy = remote(place, place, gather_send.at[n], gather_recv.at[n], links[link])
+            n = slot(half, px, pz)
+            part_n = "AB".index(half)
+            remote(block, block, gather_send.at[part_n, n], gather_recv.at[part_n, n], me).wait_recv()
+        send(task, block, lambda n: block, gather_send, gather_recv)
+
+    def send(task, src, dst, send_sem, recv_sem):
+        for one, other, key in task["sends"]:
+            part_n, n = "AB".index(key[1]), slot(*key[1:])
+            copy = remote(src, dst(n), send_sem.at[part_n, n], recv_sem.at[part_n, n], device_at(one, other))
             copy.start()
             waiting.append(copy)
 
-    def combine(task):
-        half, i, j = task["block"]
-        columns = columns_of(half, REDUCE_CUT)
-        at = (fx(i), fz(j), slice(None), columns)
-
-        def landed(n):
-            return landed_a.at[n] if half == "A" else landed_b.at[n - A_SLOTS]
-
-        slots = [REDUCE_KEYS.index(key) for key in task["deps"]]
+    def combine(half, px, pz, task):
+        columns = columns_of("reduce", half)
+        at = (fx(px), fz(pz), slice(None), columns)
+        landed = landed_a if half == "A" else landed_b
+        part_n = "AB".index(half)
+        slots = [slot(*key[1:]) for key in task["deps"]]
         for n in slots:
-            remote(landed(n), landed(n), reduce_send.at[n], reduce_recv.at[n], me).wait_recv()
+            remote(landed.at[n], landed.at[n], reduce_send.at[part_n, n], reduce_recv.at[part_n, n], me).wait_recv()
         if slots:
             total = part[at].astype(jnp.float32)
             for n in slots:
-                total = total + landed(n)[...].astype(jnp.float32)
-            if not task["sends"]:
-                total = total + hidden[:, columns].astype(jnp.float32)
-                out[:, columns] = total.astype(jnp.bfloat16)
+                total = total + landed[n].astype(jnp.float32)
+            if task["sends"]:
+                part[at] = total.astype(jnp.bfloat16)
             else:
-                part[at] = total.astype(jnp.bfloat16)
-        for link, key in task["sends"]:
-            n = REDUCE_KEYS.index(key)
-            copy = remote(part.at[at], landed(n), reduce_send.at[n], reduce_recv.at[n], links[link])
-            copy.start()
-            waiting.append(copy)
+                out[:, columns] = (total + hidden[:, columns].astype(jnp.float32)).astype(jnp.bfloat16)
+        send(task, part.at[at], lambda n: landed.at[n], reduce_send, reduce_recv)
 
     for task in plan()[0]:
         kind, *rest = task["name"]
-        if kind == "recv":
-            receive(task)
-        elif kind == "sum":
-            combine(task)
+        if kind == "gather":
+            receive(*rest, task)
+        elif kind == "reduce":
+            combine(*rest, task)
         elif kind == "cache":
             update_cache()
         else:
@@ -401,8 +397,8 @@
     return pl.pallas_call(
         layer,
         out_shape=(
-            jax.ShapeDtypeStruct(hidden.shape, jnp.bfloat16),
-            jax.ShapeDtypeStruct(cache.shape, jnp.bfloat16),
+            pltpu.VMEM(hidden.shape, jnp.bfloat16),
+            pltpu.VMEM(cache.shape, jnp.bfloat16),
         ),
         in_specs=[hbm] * 10,
         out_specs=(vmem, vmem),
@@ -415,8 +411,8 @@
             pltpu.SMEM((8,), jnp.int32),
             pltpu.VMEM((NZ, NX, ROWS, D), jnp.bfloat16),
             pltpu.VMEM((NX, NZ, ROWS, D), jnp.bfloat16),
-            pltpu.VMEM((A_SLOTS, ROWS, REDUCE_CUT), jnp.bfloat16),
-            pltpu.VMEM((len(REDUCE_KEYS) - A_SLOTS, ROWS, D - REDUCE_CUT), jnp.bfloat16),
+            pltpu.VMEM((SLOTS, ROWS, REDUCE_CUT), jnp.bfloat16),
+            pltpu.VMEM((SLOTS, ROWS, D - REDUCE_CUT), jnp.bfloat16),
             pltpu.VMEM((D, 768), jnp.bfloat16),
             pltpu.VMEM((512, D), jnp.bfloat16),
             pltpu.VMEM((2, NX + 2, NZ, ROWS, HD), jnp.bfloat16),
@@ -426,16 +422,16 @@
             pltpu.VMEM((NX, NZ, ROWS, HD), jnp.float32),
             pltpu.VMEM((NX, NZ, ROWS, HD), jnp.float32),
             pltpu.VMEM((256, 512), jnp.bfloat16),
-            dma((len(GATHER_KEYS),)),
-            dma((len(GATHER_KEYS),)),
-            dma((len(REDUCE_KEYS),)),
-            dma((len(REDUCE_KEYS),)),
+            dma((2, SLOTS)),
+            dma((2, SLOTS)),
+            dma((2, SLOTS)),
+            dma((2, SLOTS)),
             dma((NZ,)),
             dma((NZ,)),
             dma((10,)),
         ],
         compiler_params=pltpu.CompilerParams(
-            collective_id=0, has_side_effects=True, vmem_limit_bytes=63 * 1024 * 1024
+            collective_id=0, has_side_effects=True, vmem_limit_bytes=62 * 1024 * 1024
         ),
         name="layer",
     )(

time: 84.9 us -> 78.3 us (0.922)
  Pallas kernels: 80.6 us -> 75.5 us
  local copies, waits for them, and re-layouts: 3.45 us -> 1.45 us
    pallas_call x1, Pallas kernels: 80.6 us -> 75.5 us  [local(): pl.pallas_call(layer, out_shape=(pltpu.VMEM(hidden.shape, jnp.bfloat16),...]
    unnamed x2, local copies, waits for them, and re-layouts: 3.45 us -> 1.45 us
where the time goes in v3:
time: 78.3 us; the launch traced here: 77.6 us
  Pallas kernels  75.5 us (96%)
  local copies, waits for them, and re-layouts  1.45 us (2%)
    pallas_call x1, Pallas kernels, local(): pl.pallas_call(layer, out_shape=(pltpu.VMEM(hidden.shape, jnp.bfloat16),...  75.5 us

profile of v3, /device:TPU:8, one launch (start us, length us, event | category | flops | bytes accessed | tf_op | source)
XLA Modules:
  0.0 77.6 jit_solution(14744021771179610244)
XLA Ops:
  0.6 75.5 %layer.1 = (bf16[32,2048]{1,0:T(8,128)(2,1)S(1)}, bf16[16,128,128]{2,1,0:T(8,128)(2,1)S(1)}) custom-call(bf16[32,2048]{1,0:T(8,128)(2,1)} %hidden_at.1, bf16[16,128]{1,0:T(8,128)(2,1)} %bitcast.6, bf16[8,2048]{1,0:T(8,128)(2,1)} %bitcast.4, bf16[2048,128]{1,0:T(8,128)(2,1)} %kv_weight.1, bf16[2048,512]{1,0:T(8,128)(2,1)} %query_weight.1, ...), custom_call_target="tpu_custom_call" | custom-call | tf_op jit(solution)/shard_map/layer/pallas_call | solution.py:397
  76.2 0.7 copy.14
  76.8 0.8 %copy.15 = bf16[16,128,128]{2,1,0:T(8,128)(2,1)} copy(bf16[16,128,128]{2,1,0:T(8,128)(2,1)S(1)} %get-tuple-element.3) | data formatting | bytes 1048576

commit v4 on v3

--- a/solution.py
+++ b/solution.py
@@ -10,12 +10,13 @@
 
 NX, NZ, ROWS, D, HD = 4, 8, 32, 2048, 128
 EXPERTS = 4
-GATHER_CUT, REDUCE_CUT = 768, 896
 Z_OFFSETS = (0, 1, 7, 2, 6, 3, 5, 4)
 GROUPS = ((0,), (1, 7), (2, 6), (3, 5), (4,))
 ATTEND_ORDER = (2, 1, 3, 0)
 GATHER_CUT, REDUCE_CUT = 768, 896
-LINK_BYTES_PER_US, LATENCY_US = 43000.0, 2.1
+PIECES = 1
+PIECE = ROWS // PIECES
+LINK_BYTES_PER_US, LATENCY_US = 43000.0, 3.0
 FREQUENCY = [float(f) for f in (10000.0 ** (-np.arange(64, dtype=np.float32) / np.float32(64))).astype(np.float32)]
 
 RING4 = {0: (1, -1), 1: (2,)}
@@ -64,18 +65,22 @@
     for half in "AB":
         for px in range(NX):
             for pz in range(NZ):
-                own = (px, pz) == (0, 0)
-                here = ("gather", half, px, pz)
-                sends = [((px, pz), q, ("gather", half, *q)) for q in children(*here)]
-                tasks.append(dict(name=here, deps=[] if own else [here], after=[("norm",)] if own else [], sends=sends, cost=0.06))
+                for r in range(PIECES):
+                    own = (px, pz) == (0, 0)
+                    here = ("gather", half, px, pz, r)
+                    sends = [((px, pz), q, ("gather", half, *q, r)) for q in children(*here[:4])]
+                    tasks.append(
+                        dict(name=here, deps=[] if own else [here], after=[("norm",)] if own else [], sends=sends, cost=0.06)
+                    )
     for half in "AB":
         for px in ATTEND_ORDER:
             for pz in range(NZ):
-                here = ("reduce", half, px, pz)
-                deps = [("reduce", half, *q) for q in children(*here)]
-                up = parent(*here)
-                sends = [((px, pz), up, here)] if up else []
-                tasks.append(dict(name=here, deps=deps, after=[("attend", px)], sends=sends, cost=0.06))
+                for r in range(PIECES):
+                    here = ("reduce", half, px, pz, r)
+                    deps = [("reduce", half, *q, r) for q in children(*here[:4])]
+                    up = parent(*here[:4])
+                    sends = [((px, pz), up, here)] if up else []
+                    tasks.append(dict(name=here, deps=deps, after=[("attend", px)], sends=sends, cost=0.06))
     return tasks
 
 
@@ -83,7 +88,7 @@
     tasks = [dict(name=("norm",), after=[], cost=2.0)]
     tasks += [dict(name=("setup", n), after=[], cost=0.6) for n in range(4)]
     for group in GROUPS:
-        after = [("gather", half, i, j) for half in "AB" for i in range(NX) for j in group] + [("setup", n) for n in range(4)]
+        after = [("gather", half, i, j, r) for half in "AB" for i in range(NX) for j in group for r in range(PIECES)] + [("setup", n) for n in range(4)]
         tasks.append(dict(name=("project", *group), after=after, cost=0.25 + 0.75 * len(group)))
     everything = [("project", *group) for group in GROUPS]
     tasks.append(dict(name=("swap",), after=everything, cost=2.5))
@@ -120,7 +125,7 @@
         clock += task["cost"]
         for one, other, key in task.get("sends", []):
             link, hops = links_of(one, other)
-            took = ROWS * columns_in(*key[:2])[1] * 2 / LINK_BYTES_PER_US
+            took = PIECE * columns_in(*key[:2])[1] * 2 / LINK_BYTES_PER_US
             free[link] = max(clock, free.get(link, 0.0)) + took * hops
             arrived[key] = free[link] - took * (hops - 1) + LATENCY_US
         done.add(task["name"])
@@ -128,7 +133,7 @@
     return order, clock
 
 
-def slot(half, px, pz):
+def slot(px, pz):
     return px * NZ + pz - 1
 
 
@@ -148,14 +153,19 @@
     parity = lax.rem(z, 2)
     base = parity * EXPERTS
 
+    x_of = [lax.rem(x - turn * px + 2 * NX, NX) for px in range(NX)]
+    z_of = [lax.rem(z - turn * pz + 2 * NZ, NZ) for pz in range(NZ)]
+    x_steps, z_steps = [0] + [xo * NZ + z for xo in x_of[1:]], [x * NZ + zo for zo in z_of]
+
     def fx(px):
-        return lax.rem(x - turn * px + 2 * NX, NX)
+        return x_of[px % NX]
 
     def fz(pz):
-        return lax.rem(z - turn * pz + 2 * NZ, NZ)
+        return z_of[pz % NZ]
 
     def device_at(one, other):
-        return fx(one[0] - other[0]) * NZ + fz(one[1] - other[1])
+        dx, dz = (one[0] - other[0]) % NX, (one[1] - other[1]) % NZ
+        return x_steps[dx] if dx else z_steps[dz]
 
     near = [device_at((0, 0), p) for p in ((1, 0), (-1, 0), (0, 1), (0, -1), (0, 2), (0, -2))]
     partner = x * NZ + z + 1 - 2 * parity
@@ -317,13 +327,14 @@
             token = lax.broadcasted_iota(jnp.int32, (128, 640), 0) + (xa * 256 + half * 128)
             index = lax.broadcasted_iota(jnp.int32, (128, 640), 1) + ((xa - 2) * 256 + half * 128)
             allowed = (index <= token) & (index >= picks[:, 2:3].astype(jnp.int32))
-            results = []
+            shifted = []
             for n in range(2):
                 score = jnp.where(allowed, scores[n * 128 : n * 128 + 128], -1e30)
-                shifted = jnp.exp(score - jnp.max(score, axis=1, keepdims=True))
-                total = jnp.sum(shifted, axis=1, keepdims=True)
-                mean = jnp.dot(shifted.astype(jnp.bfloat16), values, preferred_element_type=jnp.float32) / total
-                results.append(mean * gates[:, n : n + 1])
+                shifted.append(jnp.exp(score - jnp.max(score, axis=1, keepdims=True)).astype(jnp.bfloat16))
+            beside = jnp.concatenate([values, jnp.ones((640, HD), jnp.bfloat16)], axis=1)
+            sums = jnp.dot(jnp.concatenate(shifted, axis=0), beside, preferred_element_type=jnp.float32)
+            mean = sums[:, 0:HD] / sums[:, HD : 2 * HD]
+            results = [mean[n * 128 : n * 128 + 128] * gates[:, n : n + 1] for n in range(2)]
             local = [picks[:, n : n + 1] - base.astype(jnp.float32) for n in range(2)]
             for e in range(EXPERTS):
                 pair = jnp.where(local[0] == float(e), results[0], jnp.where(local[1] == float(e), results[1], 0.0))
@@ -344,38 +355,41 @@
 
         lax.fori_loop(0, 16, page, 0)
 
-    def receive(half, px, pz, task):
-        block = full.at[fz(pz), fx(px), :, columns_of("gather", half)]
+    def rows_of(r):
+        return pl.ds(r * PIECE, PIECE)
+
+    def receive(half, px, pz, r, task):
+        block = full.at[fz(pz), fx(px), rows_of(r), columns_of("gather", half)]
         if task["deps"]:
-            n = slot(half, px, pz)
-            part_n = "AB".index(half)
-            remote(block, block, gather_send.at[part_n, n], gather_recv.at[part_n, n], me).wait_recv()
+            at = ("AB".index(half), r, slot(px, pz))
+            remote(block, block, gather_send.at[at], gather_recv.at[at], me).wait_recv()
         send(task, block, lambda n: block, gather_send, gather_recv)
 
     def send(task, src, dst, send_sem, recv_sem):
         for one, other, key in task["sends"]:
-            part_n, n = "AB".index(key[1]), slot(*key[1:])
-            copy = remote(src, dst(n), send_sem.at[part_n, n], recv_sem.at[part_n, n], device_at(one, other))
+            _, half, px, pz, r = key
+            at = ("AB".index(half), r, slot(px, pz))
+            copy = remote(src, dst(at[2]), send_sem.at[at], recv_sem.at[at], device_at(one, other))
             copy.start()
             waiting.append(copy)
 
-    def combine(half, px, pz, task):
-        columns = columns_of("reduce", half)
-        at = (fx(px), fz(pz), slice(None), columns)
+    def combine(half, px, pz, r, task):
+        columns, rows = columns_of("reduce", half), rows_of(r)
+        at = (fx(px), fz(pz), rows, columns)
         landed = landed_a if half == "A" else landed_b
-        part_n = "AB".index(half)
-        slots = [slot(*key[1:]) for key in task["deps"]]
+        slots = [slot(*key[2:4]) for key in task["deps"]]
         for n in slots:
-            remote(landed.at[n], landed.at[n], reduce_send.at[part_n, n], reduce_recv.at[part_n, n], me).wait_recv()
+            place, sem = landed.at[n, rows], ("AB".index(half), r, n)
+            remote(place, place, reduce_send.at[sem], reduce_recv.at[sem], me).wait_recv()
         if slots:
             total = part[at].astype(jnp.float32)
             for n in slots:
-                total = total + landed[n].astype(jnp.float32)
+                total = total + landed[n, rows].astype(jnp.float32)
             if task["sends"]:
                 part[at] = total.astype(jnp.bfloat16)
             else:
-                out[:, columns] = (total + hidden[:, columns].astype(jnp.float32)).astype(jnp.bfloat16)
-        send(task, part.at[at], lambda n: landed.at[n], reduce_send, reduce_recv)
+                out[rows, columns] = (total + hidden[rows, columns].astype(jnp.float32)).astype(jnp.bfloat16)
+        send(task, part.at[at], lambda n: landed.at[n, rows], reduce_send, reduce_recv)
 
     for task in plan()[0]:
         kind, *rest = task["name"]
@@ -422,10 +436,10 @@
             pltpu.VMEM((NX, NZ, ROWS, HD), jnp.float32),
             pltpu.VMEM((NX, NZ, ROWS, HD), jnp.float32),
             pltpu.VMEM((256, 512), jnp.bfloat16),
-            dma((2, SLOTS)),
-            dma((2, SLOTS)),
-            dma((2, SLOTS)),
-            dma((2, SLOTS)),
+            dma((2, PIECES, SLOTS)),
+            dma((2, PIECES, SLOTS)),
+            dma((2, PIECES, SLOTS)),
+            dma((2, PIECES, SLOTS)),
             dma((NZ,)),
             dma((NZ,)),
             dma((10,)),

time: 78.3 us -> 77.9 us (level)
  no operation moved by 1% of the time
where the time goes in v4:
time: 77.9 us; the launch traced here: 77.8 us
  Pallas kernels  75.7 us (97%)
  local copies, waits for them, and re-layouts  1.45 us (2%)
    pallas_call x1, Pallas kernels, local(): pl.pallas_call(layer, out_shape=(pltpu.VMEM(hidden.shape, jnp.bfloat16),...  75.7 us

profile of v4, /device:TPU:8, one launch (start us, length us, event | category | flops | bytes accessed | tf_op | source)
XLA Modules:
  0.0 77.8 jit_solution(7375673893478900918)
XLA Ops:
  0.6 75.7 %layer.1 = (bf16[32,2048]{1,0:T(8,128)(2,1)S(1)}, bf16[16,128,128]{2,1,0:T(8,128)(2,1)S(1)}) custom-call(bf16[32,2048]{1,0:T(8,128)(2,1)} %hidden_at.1, bf16[16,128]{1,0:T(8,128)(2,1)} %bitcast.6, bf16[8,2048]{1,0:T(8,128)(2,1)} %bitcast.4, bf16[2048,128]{1,0:T(8,128)(2,1)} %kv_weight.1, bf16[2048,512]{1,0:T(8,128)(2,1)} %query_weight.1, ...), custom_call_target="tpu_custom_call" | custom-call | tf_op jit(solution)/shard_map/layer/pallas_call | solution.py:411
  76.4 0.7 copy.14
  77.0 0.8 %copy.15 = bf16[16,128,128]{2,1,0:T(8,128)(2,1)} copy(bf16[16,128,128]{2,1,0:T(8,128)(2,1)S(1)} %get-tuple-element.3) | data formatting | bytes 1048576

commit v5 on v4

--- a/solution.py
+++ b/solution.py
@@ -20,6 +20,7 @@
 FREQUENCY = [float(f) for f in (10000.0 ** (-np.arange(64, dtype=np.float32) / np.float32(64))).astype(np.float32)]
 
 RING4 = {0: (1, -1), 1: (2,)}
+STAR4 = {0: (1, -1, 2)}
 CHAIN8 = {0: (1, -1), 1: (2,), 2: (3,), 3: (4,), -1: (-2,), -2: (-3,)}
 SKIP8 = {0: (1, 2, -1), 2: (3,), 3: (4,), -1: (-2,), -2: (-3,)}
 WIDE8 = {0: (1, -1, 2, -2), 2: (3, 4), -2: (-3,)}
@@ -29,8 +30,11 @@
     return {sign * p % n: tuple(sign * q % n for q in rest) for p, rest in tree.items()}
 
 
+STAR4_TURNED = turned(STAR4, NX, 1)
+
+
 def x_tree(half, pz):
-    return turned(RING4, NX, 1 if half == "A" or pz % 2 else -1)
+    return STAR4_TURNED if half == "A" else turned(RING4, NX, 1 if pz % 2 else -1)
 
 
 def z_tree(phase, half, px):
@@ -167,7 +171,7 @@
         dx, dz = (one[0] - other[0]) % NX, (one[1] - other[1]) % NZ
         return x_steps[dx] if dx else z_steps[dz]
 
-    near = [device_at((0, 0), p) for p in ((1, 0), (-1, 0), (0, 1), (0, -1), (0, 2), (0, -2))]
+    near = [device_at((0, 0), p) for p in ((1, 0), (-1, 0), (2, 0), (0, 1), (0, -1), (0, 2), (0, -2))]
     partner = x * NZ + z + 1 - 2 * parity
 
     barrier = pltpu.get_barrier_semaphore()

time: 77.9 us -> 78.6 us (level)
  no operation moved by 1% of the time
where the time goes in v5:
time: 78.6 us; the launch traced here: 78.1 us
  Pallas kernels  76 us (97%)
  local copies, waits for them, and re-layouts  1.45 us (2%)
    pallas_call x1, Pallas kernels, local(): pl.pallas_call(layer, out_shape=(pltpu.VMEM(hidden.shape, jnp.bfloat16),...  76 us

profile of v5, /device:TPU:8, one launch (start us, length us, event | category | flops | bytes accessed | tf_op | source)
XLA Modules:
  0.0 78.1 jit_solution(501442526424545311)
XLA Ops:
  0.6 76.0 %layer.1 = (bf16[32,2048]{1,0:T(8,128)(2,1)S(1)}, bf16[16,128,128]{2,1,0:T(8,128)(2,1)S(1)}) custom-call(bf16[32,2048]{1,0:T(8,128)(2,1)} %hidden_at.1, bf16[16,128]{1,0:T(8,128)(2,1)} %bitcast.6, bf16[8,2048]{1,0:T(8,128)(2,1)} %bitcast.4, bf16[2048,128]{1,0:T(8,128)(2,1)} %kv_weight.1, bf16[2048,512]{1,0:T(8,128)(2,1)} %query_weight.1, ...), custom_call_target="tpu_custom_call" | custom-call | tf_op jit(solution)/shard_map/layer/pallas_call | solution.py:415
  76.6 0.7 copy.14
  77.3 0.8 %copy.15 = bf16[16,128,128]{2,1,0:T(8,128)(2,1)} copy(bf16[16,128,128]{2,1,0:T(8,128)(2,1)S(1)} %get-tuple-element.3) | data formatting | bytes 1048576
